TPU v7x, 32 devices: a whole 2x2x4 slice. The times are simulated.
32 devices in a mesh: dp: 8 (over z, x), mp: 4 (over y, core).
Axes of the slice: x: 2, y: 2, z: 4, core: 2. Of those that a mesh axis runs over, the one named last changes fastest.
Arguments:
- tokens: bfloat16 [8, 8, 96, 768], P(None, 'dp', 'mp'), may hold values from -6 to 6
- w_qkv: bfloat16 [3, 768, 768], P(None, 'mp', 'dp'), may hold values from -0.21875 to 0.21875
- w_out: bfloat16 [768, 768], P('mp', 'dp'), may hold values from -0.625 to 0.625
- w_up: bfloat16 [3072, 768], P('mp', 'dp'), may hold values from -0.21875 to 0.21875
- w_down: bfloat16 [3072, 768], P('mp', 'dp'), may hold values from -0.109375 to 0.109375
- norm_gains: float32 [3, 768], replicated, may hold values from 0.25 to 1.75
- norm_shifts: float32 [3, 768], replicated, may hold values from -1.75 to 1.75
- branch_bias: float32 [2, 768], replicated, may hold values from -1.75 to 1.75
- qv_bias: float32 [2, 768], replicated, may hold values from -1.75 to 1.75
- up_bias: float32 [3072], replicated, may hold values from -1.75 to 1.75
- tl_in: bfloat16 [64, 768], replicated, may hold values from -0.21875 to 0.21875
- tl_bias1: float32 [64], replicated, may hold values from -1.75 to 1.75
- tl_out: bfloat16 [8, 64], replicated, may hold values from -0.75 to 0.75
- tl_bias2: float32 [8], replicated, may hold values from -3 to 3
- keep_mask: int32 [8, 96], replicated, may hold values from 0 to 1, as said below
- assign: int32 [8], replicated, may hold values from 0 to 7, each once
- cotangent: bfloat16 [8, 8, 8, 768], P('dp'), may hold values from -6 to 6
Outputs:
- pooled_out: bfloat16 [8, 8, 8, 768], P('dp')
- grad_tokens: float32 [8, 8, 96, 768], P(None, 'dp', 'mp')
- grad_qkv: float32 [3, 768, 768], P(None, 'mp', 'dp')
- grad_out: float32 [768, 768], P('mp', 'dp')
- grad_up: float32 [3072, 768], P('mp', 'dp')
- grad_down: float32 [3072, 768], P('mp', 'dp')
- grad_gains: float32 [3, 768], replicated
- grad_shifts: float32 [3, 768], replicated
- grad_branch: float32 [2, 768], replicated
- grad_qv: float32 [2, 768], replicated
- grad_upbias: float32 [3072], replicated
- grad_tl_in: float32 [64, 768], replicated
- grad_tl_bias1: float32 [64], replicated
- grad_tl_out: float32 [8, 64], replicated
- grad_tl_bias2: float32 [8], replicated
Inputs may be any that keep to these rules, and one draw needn't show every extreme that they name: `keep_mask`: every clip keeps at least one patch. `assign`: each clip appears in exactly one slot.
All inputs are finite; a program needn't handle non-finite values.
Results may differ from a plain program's by a relative error of at most 0.014.
Values may be sent and summed in bfloat16 or wider, within the bound.
No kernel may reach another device: no remote copies, remote signals or barrier semaphores. Data moves between devices by JAX's collectives and lax.ppermute only.
A program may use at most 256 MiB of HBM per device.

v0:
```python
import jax
import jax.numpy as jnp
from jax import lax
from jax.sharding import PartitionSpec as P

HD = 64
MICRO = 2


eps = 1e-06


def normalize(values, scale_vec, shift_vec):
    average = jnp.mean(values, axis=-1, keepdims=True)
    centered = values - average
    variance = jnp.mean(centered * centered, axis=-1, keepdims=True)
    return centered * lax.rsqrt(variance + eps) * scale_vec + shift_vec


def gelu_exact(values):
    return jax.nn.gelu(values, approximate=False)


def rounded(values):
    return values.astype(jnp.bfloat16)


def matmul(form, left, right):
    return jnp.einsum(form, left, right, preferred_element_type=jnp.float32)


def row_total(values):
    return jnp.sum(values.astype(jnp.float32), axis=(0, 1, 2))


def add_tuples(older, newer):
    if older is None:
        return newer
    return tuple((first_item + second_item for first_item, second_item in zip(older, newer)))


def local(
    tokens,
    w_qkv,
    w_out,
    w_up,
    w_down,
    norm_gains,
    norm_shifts,
    branch_bias,
    qv_bias,
    up_bias,
    tl_in,
    tl_bias1,
    tl_out,
    tl_bias2,
    keep_mask,
    assign,
    cotangent,
):
    column = lax.axis_index("mp")
    clips_all = tokens.shape[0]
    scale_attn = HD ** (-0.5)
    kept_all = keep_mask.astype(jnp.float32)
    arrived = lax.all_to_all(cotangent, "dp", split_axis=1, concat_axis=0, tiled=True)
    slot_table = (assign[:, None] == lax.iota(jnp.int32, clips_all)[None, :]).astype(jnp.bfloat16)
    cot_clips = rounded(matmul("sc,sfkd->cfkd", slot_table, arrived))
    patch_dev = tokens.shape[2]
    kept_patch = lax.dynamic_slice_in_dim(kept_all, column * patch_dev, patch_dev, 1)
    head_cols = w_qkv.shape[1]
    hidden_cols = w_up.shape[0]
    head_start = column * head_cols
    hidden_start = column * hidden_cols
    kept_count = jnp.sum(kept_all, axis=1)
    per_batch = clips_all // MICRO
    heads_dev = head_cols // HD
    query_bias = lax.dynamic_slice_in_dim(qv_bias[0], head_start, head_cols, 0)
    value_bias = lax.dynamic_slice_in_dim(qv_bias[1], head_start, head_cols, 0)
    proj_bias = jnp.stack([query_bias, jnp.zeros_like(query_bias), value_bias])
    up_local = lax.dynamic_slice_in_dim(up_bias, hidden_start, hidden_cols, 0)
    gathered = None
    weight_acc = None
    vector_acc = None
    pooled_parts = []
    grad_parts = []
    for batch_index in range(MICRO):
        start_clip = batch_index * per_batch
        gathered = (
            lax.all_gather(w_qkv, "dp", axis=2, tiled=True),
            lax.all_gather(w_out, "dp", axis=1, tiled=True),
            lax.all_gather(w_up, "dp", axis=1, tiled=True),
            lax.all_gather(w_down, "dp", axis=1, tiled=True),
        )
        qkv_all, out_all, up_all, down_all = gathered
        x_part = tokens[start_clip : start_clip + per_batch].astype(jnp.float32)
        kept_batch = kept_all[start_clip : start_clip + per_batch]
        kept_rows = kept_patch[start_clip : start_clip + per_batch][:, None, :, None]
        count_rows = kept_count[start_clip : start_clip + per_batch][:, None, None, None]
        cot_batch = cot_clips[start_clip : start_clip + per_batch]
        normed_one = rounded(normalize(x_part, norm_gains[0], norm_shifts[0]))
        rows_one = lax.all_gather(normed_one, "mp", axis=2, tiled=True)
        projected = rounded(
            matmul("cfpi,woi->wcfpo", rows_one, qkv_all) + proj_bias[:, None, None, None, :]
        )
        head_shape = projected.shape[1:4] + (heads_dev, HD)
        query = projected[0].reshape(head_shape)
        keys = projected[1].reshape(head_shape)
        values = projected[2].reshape(head_shape)
        key_open = kept_batch[:, None, None, None, :] > 0
        scores = jnp.where(key_open, matmul("cfphe,cfqhe->cfhpq", query, keys) * scale_attn, -1e30)
        peak_score = jnp.max(scores, axis=-1, keepdims=True)
        exponent = jnp.exp(scores - peak_score)
        denominator = jnp.sum(exponent, axis=-1, keepdims=True)
        log_total = peak_score + jnp.log(denominator)
        softmaxed = rounded(exponent / denominator)
        attended = rounded(
            matmul("cfhpq,cfqhe->cfphe", softmaxed, values).reshape(projected.shape[1:])
        )
        attn_term = matmul("cfpi,io->cfpo", attended, out_all)
        attn_out = lax.psum_scatter(attn_term, "mp", scatter_dimension=2, tiled=True)
        residual_one = x_part + attn_out + branch_bias[0]
        normed_two = rounded(normalize(residual_one, norm_gains[1], norm_shifts[1]))
        rows_two = lax.all_gather(normed_two, "mp", axis=2, tiled=True)
        hidden_pre = matmul("cfpi,hi->cfph", rows_two, up_all) + up_local
        hidden_act = rounded(gelu_exact(hidden_pre))
        mlp_term = matmul("cfph,ho->cfpo", hidden_act, down_all)
        mlp_out = lax.psum_scatter(mlp_term, "mp", scatter_dimension=2, tiled=True)
        block_out = residual_one + mlp_out + branch_bias[1]
        tl_input = rounded(normalize(block_out, norm_gains[2], norm_shifts[2]))
        tl_pre = matmul("cfpi,ti->cfpt", tl_input, tl_in) + tl_bias1
        tl_hidden = rounded(gelu_exact(tl_pre))
        map_logits = matmul("cfpt,kt->cfpk", tl_hidden, tl_out) + tl_bias2
        sigmoid_maps = jax.nn.sigmoid(map_logits)
        map_weight = rounded(sigmoid_maps) * kept_rows.astype(jnp.bfloat16)
        block_low = rounded(block_out)
        pool_term = matmul("cfpk,cfpd->cfkd", map_weight, block_low) / count_rows
        pooled = lax.psum(pool_term.astype(jnp.bfloat16), "mp").astype(jnp.float32)
        pooled_parts.append(rounded(pooled))
        grad_block = matmul("cfpk,cfkd->cfpd", map_weight, cot_batch) / count_rows
        grad_map = matmul("cfkd,cfpd->cfpk", cot_batch, block_low) / count_rows * kept_rows
        grad_logits = rounded(grad_map * sigmoid_maps * (1.0 - sigmoid_maps))
        grad_tl_out = matmul("cfpk,cfpt->kt", grad_logits, tl_hidden)
        grad_tl_bias2 = row_total(grad_logits)
        grad_tl_hidden = matmul("cfpk,kt->cfpt", grad_logits, tl_out)
        gelu_tl_pull = jax.vjp(gelu_exact, tl_pre)[1]
        grad_tl_pre = rounded(gelu_tl_pull(grad_tl_hidden)[0])
        grad_tl_in = matmul("cfpt,cfpi->ti", grad_tl_pre, tl_input)
        grad_tl_bias1 = row_total(grad_tl_pre)
        grad_tl_input = matmul("cfpt,ti->cfpi", grad_tl_pre, tl_in)
        norm_pull_three = jax.vjp(normalize, block_out, norm_gains[2], norm_shifts[2])[1]
        grad_from_norm, gain_three, shift_three = norm_pull_three(grad_tl_input)
        grad_block = grad_block + grad_from_norm
        bias_down = row_total(grad_block)
        grad_block_low = rounded(grad_block)
        grad_mlp_rows = lax.all_gather(grad_block_low, "mp", axis=2, tiled=True)
        grad_down = matmul("cfph,cfpo->ho", hidden_act, grad_mlp_rows)
        grad_hidden_act = matmul("cfpo,ho->cfph", grad_mlp_rows, down_all)
        gelu_pull = jax.vjp(gelu_exact, hidden_pre)[1]
        grad_hidden_pre = rounded(gelu_pull(grad_hidden_act)[0])
        grad_up = matmul("cfph,cfpi->hi", grad_hidden_pre, rows_two)
        grad_upbias = row_total(grad_hidden_pre)
        normed_two_term = matmul("cfph,hi->cfpi", grad_hidden_pre, up_all)
        grad_normed_two = lax.psum_scatter(
            normed_two_term.astype(jnp.bfloat16), "mp", scatter_dimension=2, tiled=True
        ).astype(jnp.float32)
        norm_pull_two = jax.vjp(normalize, residual_one, norm_gains[1], norm_shifts[1])[1]
        grad_from_two, gain_two, shift_two = norm_pull_two(grad_normed_two)
        grad_residual = grad_block + grad_from_two
        bias_attn = row_total(grad_residual)
        grad_residual_low = rounded(grad_residual)
        grad_attn_rows = lax.all_gather(grad_residual_low, "mp", axis=2, tiled=True)
        grad_out = matmul("cfpi,cfpo->io", attended, grad_attn_rows)
        grad_attended = rounded(matmul("cfpo,io->cfpi", grad_attn_rows, out_all)).reshape(
            head_shape
        )
        scores_again = jnp.where(
            key_open, matmul("cfphe,cfqhe->cfhpq", query, keys) * scale_attn, -1e30
        )
        probs_again = jnp.exp(scores_again - log_total)
        grad_probs = matmul("cfphe,cfqhe->cfhpq", grad_attended, values)
        grad_values = matmul("cfhpq,cfphe->cfqhe", rounded(probs_again), grad_attended)
        inner = jnp.sum(grad_probs * probs_again, axis=-1, keepdims=True)
        grad_scores = rounded(probs_again * (grad_probs - inner))
        grad_query = matmul("cfhpq,cfqhe->cfphe", grad_scores, keys) * scale_attn
        grad_keys = matmul("cfhpq,cfphe->cfqhe", grad_scores, query) * scale_attn
        grad_projected = rounded(
            jnp.stack([grad_query, grad_keys, grad_values]).reshape(projected.shape)
        )
        grad_qkv = matmul("wcfpo,cfpi->woi", grad_projected, rows_one)
        grad_qv_local = jnp.stack([row_total(grad_projected[0]), row_total(grad_projected[2])])
        normed_one_term = matmul("wcfpo,woi->cfpi", grad_projected, qkv_all)
        grad_normed_one = lax.psum_scatter(
            normed_one_term.astype(jnp.bfloat16), "mp", scatter_dimension=2, tiled=True
        ).astype(jnp.float32)
        norm_pull_one = jax.vjp(normalize, x_part, norm_gains[0], norm_shifts[0])[1]
        grad_from_one, gain_one, shift_one = norm_pull_one(grad_normed_one)
        grad_parts.append(grad_residual + grad_from_one)
        grad_qv_full = lax.dynamic_update_slice_in_dim(
            jnp.zeros((2, qv_bias.shape[1]), jnp.float32), grad_qv_local, head_start, 1
        )
        grad_upbias_full = lax.dynamic_update_slice_in_dim(
            jnp.zeros(up_bias.shape, jnp.float32), grad_upbias, hidden_start, 0
        )
        micro_vectors = (
            jnp.stack([gain_one, gain_two, gain_three]),
            jnp.stack([shift_one, shift_two, shift_three]),
            jnp.stack([bias_attn, bias_down]),
            grad_qv_full,
            grad_upbias_full,
            grad_tl_in,
            grad_tl_bias1,
            grad_tl_out,
            grad_tl_bias2,
        )
        vector_acc = add_tuples(vector_acc, micro_vectors)
        micro_weights = (grad_qkv, grad_out, grad_up, grad_down)
        weight_acc = add_tuples(weight_acc, micro_weights)
    weight_acc = (
        lax.psum_scatter(weight_acc[0], "dp", scatter_dimension=2, tiled=True),
        lax.psum_scatter(weight_acc[1], "dp", scatter_dimension=1, tiled=True),
        lax.psum_scatter(weight_acc[2], "dp", scatter_dimension=1, tiled=True),
        lax.psum_scatter(weight_acc[3], "dp", scatter_dimension=1, tiled=True),
    )
    pooled_here = jnp.concatenate(pooled_parts, axis=0)
    permuted = rounded(matmul("sc,cfkd->sfkd", slot_table, pooled_here))
    pooled_out = lax.all_to_all(permuted, "dp", split_axis=0, concat_axis=1, tiled=True)
    grad_whole = jnp.concatenate(grad_parts, axis=0)
    vector_sums = lax.psum(vector_acc, ("dp", "mp"))
    return (
        pooled_out,
        grad_whole,
        weight_acc[0],
        weight_acc[1],
        weight_acc[2],
        weight_acc[3],
        vector_sums[0],
        vector_sums[1],
        vector_sums[2],
        vector_sums[3],
        vector_sums[4],
        vector_sums[5],
        vector_sums[6],
        vector_sums[7],
        vector_sums[8],
    )


def solution(mesh):
    in_specs = (
        P(None, "dp", "mp", None),
        P(None, "mp", "dp"),
        P("mp", "dp"),
        P("mp", "dp"),
        P("mp", "dp"),
        P(),
        P(),
        P(),
        P(),
        P(),
        P(),
        P(),
        P(),
        P(),
        P(),
        P(),
        P("dp", None, None, None),
    )
    out_specs = (
        P("dp", None, None, None),
        P(None, "dp", "mp", None),
        P(None, "mp", "dp"),
        P("mp", "dp"),
        P("mp", "dp"),
        P("mp", "dp"),
        P(),
        P(),
        P(),
        P(),
        P(),
        P(),
        P(),
        P(),
        P(),
    )
    return jax.shard_map(local, mesh=mesh, in_specs=in_specs, out_specs=out_specs, check_vma=False)
```

profile of v0, /device:TPU:0, one launch (start us, length us, event | category | flops | bytes accessed | tf_op | source)
XLA Modules:
  0.0 691.9 jit_solution(3619782699331835735)
XLA Ops:
  16.3 32.7 %all_gather.42 = bf16[192,768]{0,1:T(8,128)(2,1)S(1)} all-gather(bf16[192,96]{0,1:T(8,128)(2,1)S(1)} %copy.121), channel_id=1, replica_groups=mesh['dp'=8,'mp'=4] {'dp'}, dimensions={1}, use_global_device_ids=true | all-gather | bytes 331776 | tf_op jit(solution)/shard_map/all_gather | solution.py:90
  49.3 7.6 %all_gather.46 = bf16[4,1,96,768]{3,2,0,1:T(8,128)(2,1)S(1)} all-gather(bf16[4,1,24,768]{3,2,0,1:T(8,128)(2,1)S(1)} %get-tuple-element.139), channel_id=1, replica_groups=mesh['dp'=8,'mp'=4] {'mp'}, dimensions={2}, use_global_device_ids=true | all-gather | bytes 737280 | tf_op jit(solution)/shard_map/all_gather | solution.py:101
  56.8 39.1 %all_gather.41 = bf16[3,192,768]{1,0,2:T(4,128)(2,1)S(1)} all-gather(bf16[3,192,96]{1,0,2:T(4,128)(2,1)S(1)} %copy.115), channel_id=1, replica_groups=mesh['dp'=8,'mp'=4] {'dp'}, dimensions={2}, use_global_device_ids=true | all-gather | bytes 995328 | tf_op jit(solution)/shard_map/all_gather | solution.py:89
  95.9 2.1 copy.116
  98.2 1.8 fusion.11
  103.9 6.8 all_gather.40
  117.2 10.5 %reduce-scatter.29.cloned.1.call-done = f32[4,1,24,768]{3,2,0,1:T(8,128)} async-done(((f32[4,1,96,768]{3,2,0,1:T(8,128)}), f32[4,1,24,768]{3,2,0,1:T(8,128)}) %reduce-scatter.29.cloned.1.call-update) | async-done | bytes 294928 | tf_op jit(solution)/shard_map/reduce_scatter | solution.py:120
  127.7 28.5 %reduce-scatter.25.cloned.1.call-done = f32[4,1,24,768]{3,2,0,1:T(8,128)} async-done(((f32[4,1,96,768]{3,2,0,1:T(8,128)}), f32[4,1,24,768]{3,2,0,1:T(8,128)}) %reduce-scatter.25.cloned.1.call-update) | async-done | bytes 294928 | tf_op jit(solution)/shard_map/reduce_scatter | solution.py:120
  158.3 7.1 %all_gather.43 = bf16[4,1,96,768]{3,2,0,1:T(8,128)(2,1)S(1)} all-gather(bf16[4,1,24,768]{3,2,0,1:T(8,128)(2,1)S(1)} %get-tuple-element.148), channel_id=1, replica_groups=mesh['dp'=8,'mp'=4] {'mp'}, dimensions={2}, use_global_device_ids=true | all-gather | bytes 737280 | tf_op jit(solution)/shard_map/all_gather | solution.py:123
  165.5 2.4 fusion.145
  169.0 3.4 multiply_convert_fusion.1
  172.4 26.8 %all-gather.5.cloned.1.call-done = bf16[768,768]{0,1:T(8,128)(2,1)} async-done(((bf16[768,96]{0,1:T(8,128)(2,1)}), bf16[768,768]{0,1:T(8,128)(2,1)}) %all-gather.5.cloned.1.call-update) | async-done | bytes 1179664 | tf_op jit(solution)/shard_map/all_gather | solution.py:92
  199.3 2.9 convolution_bitcast_fusion.4
  202.3 7.7 %all_gather.47 = bf16[4,1,96,768]{3,2,0,1:T(8,128)(2,1)S(1)} all-gather(bf16[4,1,24,768]{3,2,0,1:T(8,128)(2,1)S(1)} %get-tuple-element.149), channel_id=1, replica_groups=mesh['dp'=8,'mp'=4] {'mp'}, dimensions={2}, use_global_device_ids=true | all-gather | bytes 737280 | tf_op jit(solution)/shard_map/all_gather | solution.py:123
  210.0 2.4 fusion.146
  212.4 3.5 multiply_convert_fusion
  215.9 1.8 convolution_bitcast_fusion.2
  217.7 3.5 all-to-all-start.1
  222.1 6.3 all-to-all-done.1
  228.6 26.3 %reduce-scatter.31.cloned.1.call-done = f32[4,1,24,768]{3,2,0,1:T(8,128)} async-done(((f32[4,1,96,768]{3,2,0,1:T(8,128)}), f32[4,1,24,768]{3,2,0,1:T(8,128)}) %reduce-scatter.31.cloned.1.call-update) | async-done | bytes 294928 | tf_op jit(solution)/shard_map/reduce_scatter | solution.py:127
  263.3 7.1 %all_gather.48 = bf16[4,1,96,768]{3,2,0,1:T(8,128)(2,1)S(1)} all-gather(bf16[4,1,24,768]{3,2,0,1:T(8,128)(2,1)S(1)} %get-tuple-element.176), channel_id=1, replica_groups=mesh['dp'=8,'mp'=4] {'mp'}, dimensions={2}, use_global_device_ids=true | all-gather | bytes 737280 | tf_op jit(solution)/shard_map/all_gather | solution.py:155
  275.4 7.6 %all_gather.50 = bf16[4,1,96,768]{3,2,0,1:T(8,128)(2,1)S(1)} all-gather(bf16[4,1,24,768]{3,2,0,1:T(8,128)(2,1)S(1)} %get-tuple-element.178), channel_id=1, replica_groups=mesh['dp'=8,'mp'=4] {'mp'}, dimensions={2}, use_global_device_ids=true | all-gather | bytes 737280 | tf_op jit(solution)/shard_map/all_gather | solution.py:155
  283.1 2.4 convert_reduce_fusion
  289.5 7.1 %reduce-scatter.37.cloned.1.call-done = bf16[24,3072]{1,0:T(8,128)(2,1)} async-done(((bf16[96,3072]{1,0:T(8,128)(2,1)}), bf16[24,3072]{1,0:T(8,128)(2,1)}) %reduce-scatter.37.cloned.1.call-update) | async-done | bytes 147472
  297.9 23.2 %reduce-scatter.41.cloned.1.call-done = bf16[24,3072]{1,0:T(8,128)(2,1)} async-done(((bf16[96,3072]{1,0:T(8,128)(2,1)}), bf16[24,3072]{1,0:T(8,128)(2,1)}) %reduce-scatter.41.cloned.1.call-update) | async-done | bytes 147472
  324.5 7.5 %all_gather.51 = bf16[4,1,96,768]{3,2,0,1:T(8,128)(2,1)S(1)} all-gather(bf16[4,1,24,768]{3,2,0,1:T(8,128)(2,1)S(1)} %convert_element_type.401), channel_id=1, replica_groups=mesh['dp'=8,'mp'=4] {'mp'}, dimensions={2}, use_global_device_ids=true | all-gather | bytes 737280 | tf_op jit(solution)/shard_map/all_gather | solution.py:171
  334.2 7.7 %all_gather.49 = bf16[4,1,96,768]{3,2,0,1:T(8,128)(2,1)S(1)} all-gather(bf16[4,1,24,768]{3,2,0,1:T(8,128)(2,1)S(1)} %convert_element_type.387), channel_id=1, replica_groups=mesh['dp'=8,'mp'=4] {'mp'}, dimensions={2}, use_global_device_ids=true | all-gather | bytes 737280 | tf_op jit(solution)/shard_map/all_gather | solution.py:171
  344.0 2.4 fusion.14
  349.5 1.7 copy.146
  352.4 1.7 copy.157
  356.5 1.9 fusion.12
  363.0 1.7 fusion.13
  366.4 1.7 fusion.78
  368.2 1.9 bitcast_add_fusion.2
  370.1 4.2 copy.196
  374.3 4.7 reshape.1476
  381.0 2.1 fusion.92
  383.2 3.5 bitcast_add_fusion.1
  388.8 2.2 bitcast_add_fusion
  394.7 5.5 all-to-all-start
  400.4 7.1 %all-to-all-done = bf16[8,1,8,768]{3,2,1,0:T(8,128)(2,1)S(1)} async-done(((bf16[8,1,8,768]{3,2,1,0:T(8,128)(2,1)}), bf16[8,1,8,768]{3,2,1,0:T(8,128)(2,1)S(1)}, u32[]{:S(2)}, u32[]{:S(2)}) %all-to-all-start) | async-done | bytes 98336 | tf_op jit(solution)/shard_map/all_to_all | solution.py:226
  408.2 8.9 %reduce-scatter.47.cloned.1.call-done = f32[96,192]{1,0:T(8,128)} async-done(((f32[768,192]{1,0:T(8,128)}), f32[96,192]{1,0:T(8,128)}) %reduce-scatter.47.cloned.1.call-update) | async-done | bytes 73744
  418.8 21.9 %reduce-scatter.43.cloned.1.call-done = bf16[24,3072]{1,0:T(8,128)(2,1)} async-done(((bf16[96,3072]{1,0:T(8,128)(2,1)}), bf16[24,3072]{1,0:T(8,128)(2,1)}) %reduce-scatter.43.cloned.1.call-update) | async-done | bytes 147472
  441.8 24.1 %reduce-scatter.39.cloned.1.call-done = bf16[24,3072]{1,0:T(8,128)(2,1)} async-done(((bf16[96,3072]{1,0:T(8,128)(2,1)}), bf16[24,3072]{1,0:T(8,128)(2,1)}) %reduce-scatter.39.cloned.1.call-update) | async-done | bytes 147472
  467.7 41.8 %all-reduce = (f32[3,768]{1,0:T(4,128)}, f32[3,768]{1,0:T(4,128)}, f32[2,768]{1,0:T(2,128)}, f32[2,768]{1,0:T(2,128)}, f32[3072]{0:T(1024)}, /*index=5*/f32[64]{0:T(128)}, f32[8,64]{1,0:T(8,128)}, f32[8]{0:T(128)}) all-reduce(f32[3,768]{1,0:T(4,128)S(1)} %maximum_add_fusion, ...), channel_id=1, replica_groups=mesh['dp'=8,'mp'=4] {'dp','mp'}, use_global_device_ids=true, to_apply=%region_51.52 | all-reduce | flops 11336 | bytes 90688 | tf_op jit(solution)/shard_map/psum | solution.py:228
  510.6 26.1 %reduce-scatter.45.cloned.1.call-done = f32[96,576]{1,0:T(8,128)} async-done(((f32[768,576]{1,0:T(8,128)}), f32[96,576]{1,0:T(8,128)}) %reduce-scatter.45.cloned.1.call-update) | async-done | bytes 221200
  538.7 70.8 %reduce-scatter.33.cloned.1.call-done = f32[768,96]{0,1:T(8,128)} async-done(((f32[768,768]{0,1:T(8,128)}), f32[768,96]{0,1:T(8,128)}) %reduce-scatter.33.cloned.1.call-update) | async-done | bytes 294928 | tf_op jit(solution)/shard_map/reduce_scatter | solution.py:221
  609.5 72.3 %reduce-scatter.35.cloned.1.call-done = f32[768,96]{0,1:T(8,128)} async-done(((f32[768,768]{0,1:T(8,128)}), f32[768,96]{0,1:T(8,128)}) %reduce-scatter.35.cloned.1.call-update) | async-done | bytes 294928 | tf_op jit(solution)/shard_map/reduce_scatter | solution.py:222
  (507 shorter events, 79.4 us)
Async XLA Ops:
  8.0 248.7 %copy-start = (bf16[64,768]{1,0:T(8,128)(2,1)S(1)}, bf16[64,768]{1,0:T(8,128)(2,1)}, u32[]{:S(2)}) copy-start(bf16[64,768]{1,0:T(8,128)(2,1)} %param.27) | copy-start | bytes 294916
  8.0 41.0 %copy-start.2 = (bf16[8,1,24,768]{3,2,1,0:T(8,128)(2,1)S(1)}, bf16[8,1,24,768]{3,2,1,0:T(8,128)(2,1)}, u32[]{:S(2)}) copy-start(bf16[8,1,24,768]{3,2,1,0:T(8,128)(2,1)} %param.17) | copy-start | bytes 884740
  8.0 119.6 %reduce-scatter.29.cloned.1.call-start = ((), (), s32[]{:S(2)}) async-start(), calls=%async_computation.18 | async-start | bytes 1474560 | tf_op jit(solution)/shard_map/reduce_scatter | solution.py:120
  10.0 46.9 %copy-start.75 = (f32[4,24]{1,0:T(4,128)}, f32[4,24]{1,0:T(4,128)S(1)}, u32[]{:S(2)}) copy-start(f32[4,24]{1,0:T(4,128)S(1)} %get-tuple-element.204) | copy-start | bytes 1156
  10.0 46.9 %copy-start.77 = (f32[4,24]{1,0:T(4,128)}, f32[4,24]{1,0:T(4,128)S(1)}, u32[]{:S(2)}) copy-start(f32[4,24]{1,0:T(4,128)S(1)} %get-tuple-element.205) | copy-start | bytes 1156
  11.2 84.7 %copy-start.113 = (f32[4,24]{1,0:T(4,128)}, f32[4,24]{1,0:T(4,128)S(1)}, u32[]{:S(2)}) copy-start(f32[4,24]{1,0:T(4,128)S(1)} %get-tuple-element.81) | copy-start | bytes 1156
  11.2 84.7 %copy-start.115 = (f32[4,24]{1,0:T(4,128)}, f32[4,24]{1,0:T(4,128)S(1)}, u32[]{:S(2)}) copy-start(f32[4,24]{1,0:T(4,128)S(1)} %get-tuple-element.80) | copy-start | bytes 1156
  11.2 84.7 %copy-start.93 = (f32[4,24]{1,0:T(4,128)}, f32[4,24]{1,0:T(4,128)S(1)}, u32[]{:S(2)}) copy-start(f32[4,24]{1,0:T(4,128)S(1)} %fusion.201) | copy-start | bytes 1156
  11.2 84.7 %copy-start.95 = (f32[4,24]{1,0:T(4,128)}, f32[4,24]{1,0:T(4,128)S(1)}, u32[]{:S(2)}) copy-start(f32[4,24]{1,0:T(4,128)S(1)} %fusion.204) | copy-start | bytes 1156
  56.8 41.4 %copy-start.16 = (bf16[4,1,96,768]{3,2,0,1:T(8,128)(2,1)}, bf16[4,1,96,768]{3,2,0,1:T(8,128)(2,1)S(1)}, u32[]{:S(2)}) copy-start(bf16[4,1,96,768]{3,2,0,1:T(8,128)(2,1)S(1)} %all_gather.46) | copy-start | bytes 1769476
  103.8 52.3 %reduce-scatter.25.cloned.1.call-start = ((), (), s32[]{:S(2)}) async-start(), calls=%async_computation.14 | async-start | bytes 1474560 | tf_op jit(solution)/shard_map/reduce_scatter | solution.py:120
  114.6 50.9 %all-gather.3.cloned.1.call-start = ((), (), s32[]{:S(2)}) async-start(), calls=%async_computation.15 | async-start | bytes 1327104 | tf_op jit(solution)/shard_map/all_gather | solution.py:91
  115.2 84.1 %all-gather.5.cloned.1.call-start = ((), (), s32[]{:S(2)}) async-start(), calls=%async_computation.16 | async-start | bytes 1327104 | tf_op jit(solution)/shard_map/all_gather | solution.py:92
  115.7 112.9 %reduce-scatter.27.cloned.1.call-start = ((), (), s32[]{:S(2)}) async-start(), calls=%async_computation.17 | async-start | bytes 1474560 | tf_op jit(solution)/shard_map/reduce_scatter | solution.py:127
  157.4 10.5 %copy-start.73 = (f32[4,24]{1,0:T(4,128)}, f32[4,24]{1,0:T(4,128)S(1)}, u32[]{:S(2)}) copy-start(f32[4,24]{1,0:T(4,128)S(1)} %broadcast_multiply_fusion.4) | copy-start | bytes 1156
  172.4 29.8 %copy-start.5 = (bf16[4,96,768]{2,1,0:T(8,128)(2,1)}, bf16[4,96,768]{2,1,0:T(8,128)(2,1)S(1)}, u32[]{:S(2)}) copy-start(bf16[4,96,768]{2,1,0:T(8,128)(2,1)S(1)} %get-tuple-element.120) | copy-start | bytes 1769476
  202.2 52.7 %reduce-scatter.31.cloned.1.call-start = ((), (), s32[]{:S(2)}) async-start(), calls=%async_computation.19 | async-start | bytes 1474560 | tf_op jit(solution)/shard_map/reduce_scatter | solution.py:127
  217.6 10.8 %copy-start.134 = (s32[8]{0:T(128)S(1)}, s32[8]{0:T(128)}, u32[]{:S(2)}) copy-start(s32[8]{0:T(128)} %param.32) | copy-start | bytes 100
  217.6 37.3 %copy-start.121 = (f32[768]{0:T(1024)S(1)}, f32[768]{0:T(1024)}, u32[]{:S(2)}) copy-start(f32[768]{0:T(1024)} %get-tuple-element.98) | copy-start | bytes 9220
  217.7 10.7 %all-to-all-start.1 = ((bf16[1,8,8,768]{3,2,0,1:T(8,128)(2,1)}), bf16[1,8,8,768]{3,2,0,1:T(8,128)(2,1)S(1)}, u32[]{:S(2)}, u32[]{:S(2)}) async-start(bf16[1,8,8,768]{3,2,0,1:T(8,128)(2,1)} %bitcast.51), calls=%async_computation.5 | async-start | bytes 196608 | tf_op jit(solution)/shard_map/all_to_all | solution.py:65
  221.2 75.5 %reduce-scatter.37.cloned.1.call-start = ((), (), s32[]{:S(2)}) async-start(), calls=%async_computation.23 | async-start | bytes 737280
  222.1 35.8 %copy-start.126 = (f32[4]{0:T(128)}, f32[4]{0:T(128)S(1)}, u32[]{:S(2)}) copy-start(f32[4]{0:T(128)S(1)} %get-tuple-element.163) | copy-start | bytes 52
  222.1 37.7 %copy-start.129 = (f32[4]{0:T(128)}, f32[4]{0:T(128)S(1)}, u32[]{:S(2)}) copy-start(f32[4]{0:T(128)S(1)} %get-tuple-element.164) | copy-start | bytes 52
  262.3 12.1 %copy-start.14 = (f32[4,24,768]{2,1,0:T(8,128)}, f32[4,24,768]{2,1,0:T(8,128)S(1)}, u32[]{:S(2)}) copy-start(f32[4,24,768]{2,1,0:T(8,128)S(1)} %get-tuple-element.175) | copy-start | bytes 884740
  274.1 47.1 %reduce-scatter.41.cloned.1.call-start = ((), (), s32[]{:S(2)}) async-start(), calls=%async_computation.25 | async-start | bytes 737280
  287.7 10.1 %copy-start.120 = (f32[4,24]{1,0:T(4,128)S(1)}, f32[4,24]{1,0:T(4,128)}, u32[]{:S(2)}) copy-start(f32[4,24]{1,0:T(4,128)} %copy-done.119) | copy-start | bytes 1156
  287.7 34.4 %copy-start.102 = (f32[4,24]{1,0:T(4,128)S(1)}, f32[4,24]{1,0:T(4,128)}, u32[]{:S(2)}) copy-start(f32[4,24]{1,0:T(4,128)} %copy-done.101) | copy-start | bytes 1156
  287.8 105.1 %all-reduce.7.cloned.1.call-start = ((), (), s32[]{:S(2)}) async-start(), calls=%async_computation.29 | async-start | bytes 196608 | tf_op jit(solution)/shard_map/psum | solution.py:137
  288.7 33.8 %copy-start.118 = (f32[4,24]{1,0:T(4,128)S(1)}, f32[4,24]{1,0:T(4,128)}, u32[]{:S(2)}) copy-start(f32[4,24]{1,0:T(4,128)} %copy-done.117) | copy-start | bytes 1156
  288.7 34.1 %copy-start.100 = (f32[4,24]{1,0:T(4,128)S(1)}, f32[4,24]{1,0:T(4,128)}, u32[]{:S(2)}) copy-start(f32[4,24]{1,0:T(4,128)} %copy-done.99) | copy-start | bytes 1156
  289.5 127.7 %reduce-scatter.47.cloned.1.call-start = ((), (), s32[]{:S(2)}) async-start(), calls=%async_computation.28 | async-start | bytes 884736
  297.7 24.8 %copy-start.21 = (bf16[24,1,4,768]{3,2,1,0:T(4,128)(2,1)}, bf16[24,1,4,768]{3,2,1,0:T(4,128)(2,1)S(1)}, u32[]{:S(2)}) copy-start(bf16[24,1,4,768]{3,2,1,0:T(4,128)(2,1)S(1)} %reshape.1469) | copy-start | bytes 442372
  354.2 86.6 %reduce-scatter.43.cloned.1.call-start = ((), (), s32[]{:S(2)}) async-start(), calls=%async_computation.26 | async-start | bytes 737280
  359.9 106.0 %reduce-scatter.39.cloned.1.call-start = ((), (), s32[]{:S(2)}) async-start(), calls=%async_computation.24 | async-start | bytes 737280
  366.1 170.5 %reduce-scatter.45.cloned.1.call-start = ((), (), s32[]{:S(2)}) async-start(), calls=%async_computation.27 | async-start | bytes 2211840
  379.1 159.6 %all-reduce.5.cloned.1.call-start = ((), (), s32[]{:S(2)}) async-start(), calls=%async_computation.22 | async-start | bytes 393216 | tf_op jit(solution)/shard_map/psum | solution.py:228
  383.1 226.3 %reduce-scatter.33.cloned.1.call-start = ((), (), s32[]{:S(2)}) async-start(), calls=%async_computation.20 | async-start | bytes 2654208 | tf_op jit(solution)/shard_map/reduce_scatter | solution.py:221
  386.7 295.1 %reduce-scatter.35.cloned.1.call-start = ((), (), s32[]{:S(2)}) async-start(), calls=%async_computation.21 | async-start | bytes 2654208 | tf_op jit(solution)/shard_map/reduce_scatter | solution.py:222
  392.0 15.6 %copy-start.124 = (f32[3,64]{1,0:T(4,128)S(1)}, f32[3,64]{1,0:T(4,128)}, u32[]{:S(2)}) copy-start(f32[3,64]{1,0:T(4,128)} %get-tuple-element.186) | copy-start | bytes 2308
  392.0 74.9 %copy-start.76 = (f32[4,24]{1,0:T(4,128)S(1)}, f32[4,24]{1,0:T(4,128)}, u32[]{:S(2)}) copy-start(f32[4,24]{1,0:T(4,128)} %copy-done.75) | copy-start | bytes 1156
  392.0 74.9 %copy-start.78 = (f32[4,24]{1,0:T(4,128)S(1)}, f32[4,24]{1,0:T(4,128)}, u32[]{:S(2)}) copy-start(f32[4,24]{1,0:T(4,128)} %copy-done.77) | copy-start | bytes 1156
  392.9 74.2 %copy-start.116 = (f32[4,24]{1,0:T(4,128)S(1)}, f32[4,24]{1,0:T(4,128)}, u32[]{:S(2)}) copy-start(f32[4,24]{1,0:T(4,128)} %copy-done.115) | copy-start | bytes 1156
  392.9 74.2 %copy-start.114 = (f32[4,24]{1,0:T(4,128)S(1)}, f32[4,24]{1,0:T(4,128)}, u32[]{:S(2)}) copy-start(f32[4,24]{1,0:T(4,128)} %copy-done.113) | copy-start | bytes 1156
  392.9 74.3 %copy-start.94 = (f32[4,24]{1,0:T(4,128)S(1)}, f32[4,24]{1,0:T(4,128)}, u32[]{:S(2)}) copy-start(f32[4,24]{1,0:T(4,128)} %copy-done.93) | copy-start | bytes 1156
  392.9 74.3 %copy-start.96 = (f32[4,24]{1,0:T(4,128)S(1)}, f32[4,24]{1,0:T(4,128)}, u32[]{:S(2)}) copy-start(f32[4,24]{1,0:T(4,128)} %copy-done.95) | copy-start | bytes 1156
  394.7 12.7 %all-to-all-start = ((bf16[8,1,8,768]{3,2,1,0:T(8,128)(2,1)}), bf16[8,1,8,768]{3,2,1,0:T(8,128)(2,1)S(1)}, u32[]{:S(2)}, u32[]{:S(2)}) async-start(bf16[8,1,8,768]{3,2,1,0:T(8,128)(2,1)} %copy.134), calls=%async_computation.4 | async-start | bytes 196608 | tf_op jit(solution)/shard_map/all_to_all | solution.py:226
  400.2 109.3 %copy-start.11 = (f32[4,1,24,768]{3,2,0,1:T(8,128)S(1)}, f32[4,1,24,768]{3,2,0,1:T(8,128)}, u32[]{:S(2)}) copy-start(f32[4,1,24,768]{3,2,0,1:T(8,128)} %copy-done.10) | copy-start | bytes 884740
  509.7 174.3 %copy-start.1 = (bf16[64,768]{1,0:T(8,128)(2,1)S(1)}, bf16[64,768]{1,0:T(8,128)(2,1)}, u32[]{:S(2)}) copy-start(bf16[64,768]{1,0:T(8,128)(2,1)} %param.27) | copy-start | bytes 294916
  (115 other events, 284.5 us)
Sparse Core Ops, SparseCore 0:
  103.9 23.6 reduce-scatter.28
  130.4 25.7 reduce-scatter.24
  202.4 24.1 reduce-scatter.26
  229.2 25.7 reduce-scatter.30
  274.2 22.4 reduce-scatter.36
  299.0 22.0 reduce-scatter.40
  324.0 31.4 all-reduce.6
  387.0 127.1 all-reduce.4
Sparse Core Ops, SparseCore 1:
  117.2 39.9 all-gather.2
  159.3 40.0 all-gather.4
  354.2 62.9 reduce-scatter.46
  419.7 21.0 reduce-scatter.42
  443.8 22.0 reduce-scatter.38
  469.4 67.2 reduce-scatter.44
  541.0 68.4 reduce-scatter.32
  613.8 67.9 reduce-scatter.34
where the time goes:
time: 701 us; the launch traced here: 692 us
  waiting for transfers between devices  361 us (51%)
  blocking collectives  173 us (25%)
  matrix products  56.8 us (8%)
  local copies, waits for them, and re-layouts  53 us (8%)
  other arithmetic  19.9 us (3%)
  between operations  18.3 us (3%)
  starting transfers between devices  9.92 us (1%)
    unnamed x22, waiting for transfers between devices  113 us
    reduce_scatter x1, waiting for transfers between devices, local(): lax.psum_scatter(weight_acc[3], 'dp', scatter_dimension=1, tiled=True)  72.3 us
    reduce_scatter x1, waiting for transfers between devices, local(): lax.psum_scatter(weight_acc[2], 'dp', scatter_dimension=1, tiled=True)  70.8 us
    dot_general x56, matrix products, matmul(): return jnp.einsum(form, left, right, preferred_element_type=jnp.float32)  56.8 us
    psum x1, blocking collectives, local(): vector_sums = lax.psum(vector_acc, ('dp', 'mp'))  41.8 us
    all_gather x1, blocking collectives, local(): lax.all_gather(w_qkv, 'dp', axis=2, tiled=True)  39.1 us
    reduce_scatter x2, waiting for transfers between devices, local(): lax.psum_scatter(attn_term, 'mp', scatter_dimension=2, tiled=True)  39 us
    unnamed x312, local copies, waits for them, and re-layouts  35.9 us
  transfers between devices with their start and end apart: 18, of which 14 were waited for; matrix products, arithmetic and copies ran while one was open for 13% of the time, Pallas kernels for 0%

commit v1 on v0

v1 whole, which is shorter than its diff:
```python
import functools

import jax
import jax.numpy as jnp
from jax import lax
from jax.experimental import pallas as pl
from jax.experimental.pallas import tpu as pltpu
from jax.sharding import PartitionSpec as P

HD = 64
GROUP = 4
EPS = 1e-06
DOWN = (1, 2, 4)
P1_STEPS = 2
OWN_FIRST = 1
F32 = jnp.float32
BF16 = jnp.bfloat16
COST = {"chip_sum": 4, "ffn_fwd_other": 4, "attn_fwd_own": 4, "pair_second": 0.3, "join": 8, "prep": 0.3, "ffn_fwd_own": 8, "turn": 8, "pair_first": 0.3, "attn_fwd_other": 2, "token_sum": 0.05, "down_grads": 4, "finish": 0.05, "attn_bwd": 16, "attn_grads": 4, "mid_back": 8, "up_grads": 40, "owner_first": 0.3, "turned_sum": 0.3, "learner": 8, "owner_second": 2, "token_bwd": 40, "add_last": 0.3, "early_sum": 0.3, "ffn_bwd_own": 0.05}
ORDER = {"up": (2, 4, 1), "first": (1, 2, 4), "second": (1, 2, 4)}
WAITS = {
    "gate_up": ("wa_n", "own_x",),
    "join_up": ("wa_x0", "wa_z",),
    "gate_down": ("up_n",),
    "attn_fwd_other": ("up_n", "own_x",),
    "attn_fwd_own": ("up_z", "down_n",),
    "chip_sum_0": ("down_n",),
    "join_down": ("wa_x1",),
    "chip_sum_2": ("down_send",),
    "mid_back": ("up_send",),
    "attn_grads": ("down_second",),
    "token_sum": ("first_first", "up_first",),
    "down_second": ("attn_send",),
    "up_first": ("down_first",),
    "up_second": ("attn_send",),
    "token_bwd": ("attn_send",),
    "early_sum": ("first_first",),
    "down_last": ("first_second",),
    "fold": ("first_first",),
    "attn_bwd": ("up_send",),
    "token_last": ("second_second", "first_second",),
    "second_first": ("first_first",),
    "pool_last": ("second_second", "up_second",),
}


def swap(values, axis, bit):
    size = lax.axis_size(axis)
    return lax.ppermute(values, axis, [(i, i ^ bit) for i in range(size)])


def split_axis():
    return lax.axis_size("dp") == 8


def swap_dp(values, bit):
    return swap(values, "dp", bit) if split_axis() else jnp.zeros_like(values)


def dot(left, right):
    return lax.dot_general(left, right, (((1,), (0,)), ((), ())), preferred_element_type=F32)


def dot_nt(left, right):
    return lax.dot_general(left, right, (((1,), (1,)), ((), ())), preferred_element_type=F32)


def dot_tn(left, right):
    return lax.dot_general(left, right, (((0,), (0,)), ((), ())), preferred_element_type=F32)


def gelu_parts(x):
    z = jnp.abs(x) * 0.7071067811865476
    t = 1.0 / (1.0 + 0.3275911 * z)
    bell = jnp.exp(-(z * z))
    series = t * (0.127414796 + t * (-0.142248368 + t * (0.7107068705 + t * (-0.7265760135 + t * 0.5307027145))))
    tail = series * bell
    cdf = jnp.where(x < 0, tail, 1.0 - tail)
    return x * cdf, cdf + x * bell * 0.3989422804014327


def norm_stats(v):
    mean = jnp.mean(v, axis=-1, keepdims=True)
    centered = v - mean
    var = jnp.mean(centered * centered, axis=-1, keepdims=True)
    rstd = lax.rsqrt(var + EPS)
    return centered * rstd, rstd


def norm_back(grad, xhat, rstd, gain):
    scaled = grad * gain
    first = jnp.mean(scaled, axis=-1, keepdims=True)
    second = jnp.mean(scaled * xhat, axis=-1, keepdims=True)
    return (scaled - first - xhat * second) * rstd


def place(parts, order, me_dp, target):
    for part, partners in zip(parts, order):
        rows = part.shape[0] // len(partners)
        for i, j in enumerate(partners):
            if len(order) == 1:
                target[...] = part[...]
            elif j is not None:
                at = pl.ds(pl.multiple_of((me_dp ^ j) * rows, 32), rows)
                target[at, :] = part[i * rows : (i + 1) * rows, :]


def position():
    return lax.axis_index("mp"), lax.axis_index("dp")


def rowsum(v):
    return jnp.sum(v, axis=0, keepdims=True)


def put_halves(target, start, v):
    high = v.astype(BF16)
    rows = v.shape[0]
    target[start : start + rows, :] = high
    target[start + rows : start + 2 * rows, :] = (v - high.astype(F32)).astype(BF16)


def get_halves(source, start, rows):
    return source[start : start + rows, :].astype(F32) + source[start + rows : start + 2 * rows, :].astype(F32)


def head_masks(shape):
    lanes = lax.broadcasted_iota(jnp.int32, shape, 1)
    return [(lanes >= HD * h) & (lanes < HD * (h + 1)) for h in range(shape[1] // HD)]


def stack_heads(v, masks):
    zero = jnp.zeros_like(v)
    return jnp.concatenate([jnp.where(m, v, zero) for m in masks], axis=0)


def merge_heads(stacked, masks):
    rows = masks[0].shape[0]
    out = stacked[0:rows, :]
    for h in range(1, len(masks)):
        out = jnp.where(masks[h], stacked[h * rows : (h + 1) * rows, :], out)
    return out


def join(n, *refs):
    start = 0
    for ref in refs[:n]:
        refs[-1][start : start + ref.shape[0], :] = ref[...]
        start += ref.shape[0]


def turn(first, second, out):
    out[...] = jnp.concatenate([first[...].astype(F32), second[...].astype(F32)], axis=0).T.astype(BF16)


def gate(value, *rest):
    rest[-1][...] = value[...]


def prep(cfg, *refs):
    sc = position()
    G, half, b = cfg
    gains, shifts = refs[4:6]
    x_other, x_own, n_other, n_own, xs = refs[-5:]
    me = sc[0]
    core = me & 1
    for side in (0, 1):
        cside = core if side else 1 - core
        for j in range(4):
            at = pl.ds(pl.multiple_of((cside * half + b * G) * 24, 48), G * 24)
            xs[side * G : (side + 1) * G, me ^ j] = refs[j][at, :].astype(F32).reshape(G, 24, -1)
    gain, shift = gains[0:1, :], shifts[0:1, :]
    for side, x_out, n_out in ((0, x_other, n_other), (1, x_own, n_own)):

        def step(r, carry):
            v = xs[side * G + r].reshape(96, -1)
            at = pl.ds(pl.multiple_of(r * 96, 96), 96)
            x_out[at, :] = v.astype(BF16)
            xhat, _ = norm_stats(v)
            n_out[at, :] = (xhat * gain + shift).astype(BF16)
            return carry

        lax.fori_loop(0, G, step, 0)


def attn_fwd(cfg, *refs):
    sc = position()
    G, half, b, side, order, n_dep = cfg
    n1, keep, bias = refs[0:3]
    n_w = len(order) if order else 1
    w_in = refs[3 : 3 + n_w]
    outs = refs[3 + n_w + n_dep :]
    q_out, k_out, v_out, att, probs, part = outs[:6]
    me, me_dp = sc[0], sc[1]
    core = me & 1
    hcol = att.shape[1]
    heads = hcol // HD
    if order:
        wa = outs[6]
        place(w_in, order, me_dp, wa)
    else:
        wa = w_in[0]
    for w, out in enumerate((q_out, k_out, v_out)):
        t = dot(n1[...], wa[:, w * hcol : (w + 1) * hcol])
        if w != 1:
            row = w // 2
            for m in range(bias.shape[1] // hcol):
                t = t + jnp.where(me == m, bias[row : row + 1, m * hcol : (m + 1) * hcol], 0.0)
        out[...] = t.astype(BF16)
    masks = head_masks((96, hcol))
    clip0 = (core if side else 1 - core) * half + b * G

    def attend(i, carry):
        for r in (2 * i, 2 * i + 1):
            at = pl.ds(pl.multiple_of(r * 96, 96), 96)
            open_row = keep[pl.ds(clip0 + r, 1), :] > 0
            s = dot_nt(stack_heads(q_out[at, :], masks), k_out[at, :]) * HD ** (-0.5)
            s = jnp.where(open_row, s, -1e30)
            e = jnp.exp(s - jnp.max(s, axis=-1, keepdims=True))
            p = (e * (1.0 / jnp.sum(e, axis=-1, keepdims=True))).astype(BF16)
            probs[pl.ds(pl.multiple_of(r * heads * 96, 96), heads * 96), :] = p
            att[at, :] = merge_heads(dot(p, v_out[at, :]), masks).astype(BF16)
        return carry

    lax.fori_loop(0, G // 2, attend, 0, unroll=True)
    part[...] = dot_nt(att[...], wa[:, 3 * hcol : 4 * hcol]).astype(part.dtype)


def chip_sum(part, came, *rest):
    rest[-1][...] = (part[...] + came[...].astype(F32)).astype(BF16)


def mid_norm(mine, came, x, branch, gains, shifts, *rest):
    res, n2 = rest[-2:]
    v = x[...].astype(F32) + (mine[...].astype(F32) + came[...].astype(F32)) + branch[0:1, :]
    res[...] = v
    xhat, _ = norm_stats(v)
    n2[...] = (xhat * gains[1:2, :] + shifts[1:2, :]).astype(BF16)


def ffn_fwd(orders, *refs):
    sc = position()
    n2, bias = refs[0:2]
    if orders:
        n_up, n_w = len(orders[0]), len(orders[0]) + len(orders[1])
        act, slope, part, wu, wd = refs[2 + n_w :]
        place(refs[2 : 2 + n_up], orders[0], sc[1], wu)
        place(refs[2 + n_up : 2 + n_w], orders[1], sc[1], wd)
    else:
        wu, wd, act, slope, part = refs[2:]
    hid = wu.shape[1]
    row_bias = bias[:, pl.ds(pl.multiple_of(sc[0] * hid, 128), hid)]
    tile = 256
    for c in range(hid // tile):
        at = slice(c * tile, (c + 1) * tile)
        pre = dot(n2[...], wu[:, at]) + row_bias[:, at]
        g, d = gelu_parts(pre)
        act[:, at] = g.astype(BF16)
        slope[:, at] = d.astype(BF16)
    part[...] = dot_nt(act[...], wd[...]).astype(part.dtype)


def learner(cfg, assign, *refs):
    sc = position()
    G, half, b, n_cot, ride = cfg
    res, mine, came, branch, gains, shifts, tl_in, tl_b1, tl_out, tl_b2, keep = refs[:11]
    cots = refs[11 : 11 + n_cot]
    grad, grad_low, vec = refs[11 + n_cot : 14 + n_cot]
    R = G * 96
    me_dp = sc[1]
    core = sc[0] & 1
    if n_cot > 1:
        cot = refs[14 + n_cot]
        cot[0:2] = cots[0][0:2]
        cot[2:4] = cots[1][0:2]
        cot[4:8] = cots[2][...]
    else:
        cot = cots[0]
    block = res[...] + (mine[...].astype(F32) + came[...].astype(F32)) + branch[1:2, :]
    low = block.astype(BF16)
    xhat, rstd = norm_stats(block)
    gain = gains[2:3, :]
    tl_x = (xhat * gain + shifts[2:3, :]).astype(BF16)
    pre = dot_nt(tl_x, tl_in[...]) + tl_b1[...]
    hid, slope = gelu_parts(pre)
    hid = hid.astype(BF16)
    logits = dot_nt(hid, tl_out[...]) + tl_b2[...]
    sig = 1.0 / (1.0 + jnp.exp(-logits))
    sig_low = sig.astype(BF16).astype(F32)
    eye = lax.broadcasted_iota(jnp.int32, (96, 96), 0) == lax.broadcasted_iota(jnp.int32, (96, 96), 1)
    pieces, g_maps, pooled = [], [], []
    for g in range(G):
        clip = core * half + b * G + g
        rows = slice(g * 96, (g + 1) * 96)
        keep_row = keep[pl.ds(clip, 1), :].astype(F32)
        inv = 1.0 / jnp.sum(keep_row, axis=1, keepdims=True)
        keep_col = jnp.sum(jnp.where(eye, keep_row, 0.0), axis=1, keepdims=True)
        weight = (sig_low[rows, :] * keep_col).astype(BF16)
        pooled.append(dot_tn(weight, low[rows, :]) * inv)
        at_slot = lax.fori_loop(
            0, assign.shape[0], lambda i, found: jnp.where(assign[i] == clip, i, found), 0, unroll=assign.shape[0] <= 8
        )
        c = cot[at_slot ^ me_dp] if n_cot > 1 else cot[at_slot]
        pieces.append(dot(weight, c) * inv)
        g_maps.append(dot_nt(low[rows, :], c) * inv * keep_col)
    g_map = jnp.concatenate(g_maps, axis=0)
    g_logits = g_map * sig * (1.0 - sig)
    g_low = g_logits.astype(BF16)
    g_hid = dot(g_low, tl_out[...])
    g_pre = (g_hid * slope).astype(BF16)
    g_x = dot(g_pre, tl_in[...])
    total = jnp.concatenate(pieces, axis=0) + norm_back(g_x, xhat, rstd, gain)
    grad[...] = total
    grad_low[0:R, :] = total.astype(BF16)
    grad_low[R : R + 8 * G, :] = jnp.concatenate(pooled, axis=0).astype(BF16)
    hidden = tl_in.shape[0]
    vec[...] = jnp.zeros_like(vec)
    vec[0:hidden, :] = dot_tn(g_pre, tl_x)
    vec[hidden : hidden + 8, 0:hidden] = dot_tn(g_low, hid)
    vec[hidden + 8 : hidden + 9, :] = rowsum(g_x * xhat)
    vec[hidden + 9 : hidden + 10, :] = rowsum(g_x)
    vec[hidden + 10 : hidden + 11, :] = rowsum(total)
    vec[hidden + 11 : hidden + 12, 0:hidden] = rowsum(g_pre.astype(F32))
    vec[hidden + 12 : hidden + 13, 0:8] = rowsum(g_low.astype(F32))
    if ride:
        put_halves(grad_low, R + 8 * G, vec[...])


def ffn_bwd(n_vec, g, slope, wu, wd, *refs):
    part, g_pre, up_sum = refs[n_vec:]
    hid = wu.shape[1]
    R = slope.shape[0]
    tile = 256
    for c in range(hid // tile):
        at = slice(c * tile, (c + 1) * tile)
        v = (dot(g[0:R, :], wd[:, at]) * slope[:, at].astype(F32)).astype(BF16)
        g_pre[:, at] = v
        total = rowsum(v.astype(F32))
        up_sum[:, at] = total + refs[0][:, at] if n_vec else total
    part[...] = dot_nt(g_pre[...], wu[...]).astype(part.dtype)


def partner(order, k):
    return (k >> 1) * order[1] + (k & 1) * order[2]


def weight_grads(cfg, *refs):
    sc = position()
    n_left, n_right, widths, terms_of, cuts, extra, n_extra_in, n_dep = cfg
    lefts, rights = refs[:n_left], refs[n_left : n_left + n_right]
    more = refs[n_left + n_right : n_left + n_right + n_extra_in]
    outs, acc = refs[n_left + n_right + n_extra_in + n_dep : -1], refs[-1]
    n_out = 2 * len(cuts) if cuts else 1
    me_dp = sc[1]
    rows = acc.shape[0]
    tile = 256

    def step(m, carry):
        at = pl.ds(pl.multiple_of(m * tile, tile), tile)
        start = 0
        for width, terms in zip(widths, terms_of):
            total = None
            for left, right in terms:
                n = rights[right].shape[0]
                term = dot_tn(lefts[left][0:n, at], rights[right][...])
                total = term if total is None else total + term
            acc[at, start : start + width] = total
            start += width
        return carry

    lax.fori_loop(0, rows // tile, step, 0, unroll=True)
    if not cuts:
        outs[0][...] = acc[...]
    else:
        size = rows // 8
        start = 0
        for c, (width, order) in enumerate(cuts):
            for k in range(4):
                at = slice(k * size, (k + 1) * size)
                j = partner(order, k)
                far = pl.ds(pl.multiple_of((me_dp ^ j ^ order[0]) * size, 32), size)
                near = pl.ds(pl.multiple_of((me_dp ^ j) * size, 32), size)
                outs[2 * c][at, :] = acc[far, start : start + width].astype(BF16)
                outs[2 * c + 1][at, :] = acc[near, start : start + width]
            start += width
    if extra is not None:
        extra(sc, more, outs[:n_out], outs[n_out:], acc, rights)


def ride_down(half, R, G, sc, more, sent, outs, acc, rights):
    assign, low_own, low_other = more
    me_dp, core = sc[1], sc[0] & 1
    rows = sent[1].shape[0]
    for k in range(4):
        found = []
        for j in (partner(DOWN, k) + DOWN[0], partner(DOWN, k)):
            clip = assign[me_dp ^ j]
            inside = jnp.where(clip < half, clip, clip - half)
            at = pl.ds(pl.multiple_of(R + 8 * inside, 8), 8)
            mine = jnp.where(clip < half, 0, 1) == core
            found.append(jnp.where(mine, low_own[at, :].astype(F32), low_other[at, :].astype(F32)))
        outs[0][8 * k : 8 * k + 8, :] = found[0]
        outs[0][32 + 8 * k : 40 + 8 * k, :] = found[1]
    sent[0][rows : rows + 32, :] = outs[0][0:32, :].astype(BF16)
    quarter = outs[1].shape[0] // 2
    n_vec = 4 * quarter
    total = get_halves(low_own, R + 8 * G, n_vec) + get_halves(low_other, R + 8 * G, n_vec)
    mine = total[0:quarter, :]
    for m in (1, 2, 3):
        mine = jnp.where(sc[0] == m, total[m * quarter : (m + 1) * quarter, :], mine)
    put_halves(outs[1], 0, mine)
    sent[0][rows + 32 : rows + 32 + 2 * quarter, :] = outs[1][...]


def lane_total(v):
    full = v.shape[1] // 128
    total = sum(v[:, 128 * k : 128 * (k + 1)] for k in range(full))
    rest = v.shape[1] - 128 * full
    if rest:
        total = total + jnp.concatenate([v[:, 128 * full :], jnp.zeros((v.shape[0], 128 - rest), F32)], axis=1)
    return rowsum(total.T)


def late_vectors(sc, more, sent, outs, acc, rights):
    wa, gains, shifts, mid_vec, up_sum = more
    vec = outs[-1]
    me = sc[0]
    hcol = wa.shape[1] // 4
    n = len(rights) // 4
    sums = [sum(rowsum(r[...].astype(F32)) for r in rights[w * n : (w + 1) * n]) for w in range(3)]
    row = jnp.concatenate(sums, axis=1)
    vec[...] = jnp.zeros_like(vec)
    vec[0:3, :] = 0.5 * mid_vec[0:3, :]
    for c in range(acc.shape[0] // 256):
        at = slice(256 * c, 256 * (c + 1))
        weight = wa[at, 0 : 3 * hcol].astype(F32)
        shift_grad = lane_total(weight * row)
        vec[3:4, at] = (lane_total(weight * acc[at, 0 : 3 * hcol]) - shifts[0:1, at] * shift_grad) / gains[0:1, at]
        vec[4:5, at] = shift_grad
    vec[pl.ds(5 + me, 1), :] = up_sum[...]
    vec[pl.ds(9 + me, 1), 0:hcol] = sums[0]
    vec[pl.ds(9 + me, 1), 256 : 256 + hcol] = sums[2]
    if len(outs) > 1:
        half = vec.shape[1] // 2
        put_halves(outs[0], 0, jnp.concatenate([vec[:, 0:half], vec[:, half:]], axis=0))
        rows = acc.shape[0] // 2
        sent[0][rows : rows + outs[0].shape[0], :] = outs[0][...]


def mid_back(mine, came, res, grad_block, gains, *rest):
    grad, grad_low, vec = rest[-3:]
    g = mine[...].astype(F32) + came[...].astype(F32)
    xhat, rstd = norm_stats(res[...])
    total = grad_block[...] + norm_back(g, xhat, rstd, gains[1:2, :])
    grad[...] = total
    grad_low[...] = total.astype(BF16)
    vec[...] = jnp.zeros_like(vec)
    vec[0:1, :] = rowsum(g * xhat)
    vec[1:2, :] = rowsum(g)
    vec[2:3, :] = rowsum(total)


def attn_bwd(n_dep, g_own, g_other, *refs):
    own, other = refs[0:4], refs[4:8]
    wa = refs[8]
    outs = refs[9 + n_dep :]
    g_att = outs[6]
    R, hcol = own[0].shape
    heads = hcol // HD
    scale = HD ** (-0.5)
    masks = head_masks((96, hcol))
    for g, (q, k, v, probs), (gq, gk, gv) in ((g_own, own, outs[0:3]), (g_other, other, outs[3:6])):
        g_att[...] = dot(g[...], wa[:, 3 * hcol : 4 * hcol]).astype(BF16)

        def attend(i, carry):
            for r in (2 * i, 2 * i + 1):
                at = pl.ds(pl.multiple_of(r * 96, 96), 96)
                gs = stack_heads(g_att[at, :], masks)
                qs = stack_heads(q[at, :], masks)
                p = probs[pl.ds(pl.multiple_of(r * heads * 96, 96), heads * 96), :]
                pf = p.astype(F32)
                gp = dot_nt(gs, v[at, :])
                inner = jnp.sum(gp * pf, axis=-1, keepdims=True)
                ds = (pf * (gp - inner)).astype(BF16)
                gv[at, :] = dot_tn(p, gs).astype(BF16)
                gq[at, :] = (merge_heads(dot(ds, k[at, :]), masks) * scale).astype(BF16)
                gk[at, :] = (dot_tn(ds, qs) * scale).astype(BF16)
            return carry

        lax.fori_loop(0, R // 192, attend, 0, unroll=True)


def token_bwd(cfg, *refs):
    G, n_dep = cfg
    own, other = refs[0:4], refs[4:8]
    wa, gains, grad_res = refs[8:11]
    near_other, near_own, far, xs, gn_all = refs[11 + n_dep :]
    me = position()[0]
    hcol = own[0].shape[1]
    gain = gains[0:1, :]
    tile = 256
    for side, (gq, gk, gv, x), near in ((1, own, near_own), (0, other, near_other)):

        def spread(c, carry):
            at = pl.ds(pl.multiple_of(c * tile, tile), tile)
            gn_all[:, at] = sum(dot_nt(t[...], wa[at, w * hcol : (w + 1) * hcol]) for w, t in enumerate((gq, gk, gv)))
            return carry

        lax.fori_loop(0, gn_all.shape[1] // tile, spread, 0)

        def back(r, carry):
            at = pl.ds(pl.multiple_of(r * 96, 96), 96)
            gn = gn_all[at, :]
            xhat, rstd = norm_stats(x[at, :].astype(F32))
            gx = norm_back(gn, xhat, rstd, gain)
            if side:
                gx = gx + 0.5 * grad_res[at, :]
            xs[r] = gx.reshape(4, 24, -1)
            return carry

        lax.fori_loop(0, G, back, 0)
        start = 0 if side else 2 * G * 24
        for n in (0, 1):
            near[n * G * 24 : (n + 1) * G * 24, :] = xs[:, me ^ (2 * n)].reshape(G * 24, -1)
            far[start + n * G * 24 : start + (n + 1) * G * 24, :] = (
                xs[:, me ^ (2 * n + 1)].reshape(G * 24, -1).astype(BF16)
            )


def token_sum(near_other, near_own, came, *refs):
    keep, go = refs[-2:]
    core = position()[0] & 1
    size = near_own.shape[0] // 2
    for cside, near, first in ((1 - core, near_other, 0), (core, near_own, 2 * size)):
        at = pl.ds(pl.multiple_of(cside * size, 48), size)
        keep[at, :] = near[0:size, :] + came[first : first + size, :].astype(F32)
        go[at, :] = (near[size:, :] + came[first + size : first + 2 * size, :].astype(F32)).astype(BF16)


def fold(own, came, *refs):
    out = refs[-1]
    n = own.shape[0] - 16
    out[0:n, :] = own[0:n, :].astype(BF16)
    out[n : 2 * n, :] = came[0:n, :].astype(BF16)
    put_halves(out, 2 * n, own[n:, :] + came[n:, :])


def owner_first(ride, came, own, *refs):
    n = own.shape[0] // 2
    if ride:
        kept, early = refs[0:2]
        go, keep, stay, early_out = refs[-4:]
        put_halves(early_out, 0, get_halves(early, 0, early.shape[0] // 2) + get_halves(came, 2 * n + 32, early.shape[0] // 2))
        for k in range(4):
            out, at = (stay, 16 * k) if k < 2 else (go, n + 16 * (k - 2))
            out[at : at + 8, :] = kept[32 + 8 * k : 40 + 8 * k, :].astype(BF16)
            out[at + 8 : at + 16, :] = came[2 * n + 8 * k : 2 * n + 8 * k + 8, :]
        go[n + 32 :, :] = early_out[...]
    else:
        go, keep = refs[-2:]
    go[0:n, :] = (own[n : 2 * n, :] + came[n : 2 * n, :].astype(F32)).astype(BF16)
    keep[...] = own[0:n, :] + came[0:n, :].astype(F32)


def owner_second(ride, came, own, *refs):
    n = own.shape[0] // 2
    if ride:
        stay, early = refs[0:2]
        go, keep, early_out = refs[-3:]
        rows = early.shape[0] // 2
        early_out[...] = (get_halves(early, 0, rows) + get_halves(came, 2 * n + 32, rows)).astype(BF16)
        go[n : n + 16, :] = stay[16:32, :]
        go[n + 16 : n + 32, :] = came[2 * n + 16 : 2 * n + 32, :]
        go[n + 32 :, :] = early_out[...]
    else:
        go, keep = refs[-2:]
    go[0:n, :] = (own[n:, :] + came[n : 2 * n, :].astype(F32)).astype(BF16)
    keep[...] = own[0:n, :] + came[0:n, :].astype(F32)


def late_first(came, own, late, *refs):
    go, keep, late_out = refs[-3:]
    n = own.shape[0] // 2
    rows = late.shape[0] // 2
    put_halves(late_out, 0, get_halves(late, 0, rows) + get_halves(came, 2 * n, rows))
    go[0:n, :] = (own[n : 2 * n, :] + came[n : 2 * n, :].astype(F32)).astype(BF16)
    go[n:, :] = late_out[...]
    keep[...] = own[0:n, :] + came[0:n, :].astype(F32)


def late_second(came, own, late, *refs):
    go, keep, late_out = refs[-3:]
    n = own.shape[0] // 2
    rows = late.shape[0] // 2
    late_out[...] = (get_halves(late, 0, rows) + get_halves(came, 2 * n, rows)).astype(BF16)
    go[0:n, :] = (own[n:, :] + came[n : 2 * n, :].astype(F32)).astype(BF16)
    go[n:, :] = late_out[...]
    keep[...] = own[0:n, :] + came[0:n, :].astype(F32)


def early_sum(own, came, late, late_came, *refs):
    out = refs[-1]
    n = own.shape[0]
    out[0:n, :] = own[...].astype(F32) + came[came.shape[0] - n :, :].astype(F32)
    rows, half = late.shape
    total = late[...].astype(F32) + late_came[late_came.shape[0] - rows :, :].astype(F32)
    out[n:, 0:half] = total[0 : rows // 2, :]
    out[n:, half:] = total[rows // 2 :, :]


def add_last(own, came, *refs):
    out = refs[-1]
    out[...] = own[...] + came[0 : own.shape[0], :].astype(F32)


def turned_sum(n, *refs):
    outs = refs[2 * n :]
    pieces = []
    for i in range(n):
        own, came = refs[2 * i : 2 * i + 2]
        total = own[...] + came[0 : own.shape[0], :].astype(F32)
        pieces.append(total.T)
    at = 0
    flat = pieces[0] if n == 1 else jnp.concatenate(pieces, axis=0)
    for out in outs:
        out[...] = flat[at : at + out.shape[0], :]
        at += out.shape[0]


def cot_first(cot, *refs):
    sc = position()
    far, near = refs[-2:]
    me_dp = sc[1]
    for k in range(4):
        far[k] = cot[me_dp ^ (2 * k + 1)]
        near[k] = cot[me_dp ^ (2 * k)]


def pair_first(near, came, go, stay):
    for i, k in enumerate((1, 3)):
        go[2 * i] = near[k]
        go[2 * i + 1] = came[k]
        stay[2 * i] = near[k - 1]
        stay[2 * i + 1] = came[k - 1]


def pair_second(stay, came, go):
    go[0:2] = stay[2:4]
    go[2:4] = came[2:4]


def pool_last(at, stay, one, two, *refs):
    out = refs[-1]
    me_dp = position()[1]
    for j in range(8):
        rows = (stay[8 * j : 8 * j + 8, :] if j < 2 else one[at[0] + 8 * j - 16 : at[0] + 8 * j - 8, :] if j < 4
                else two[at[1] + 8 * j - 32 : at[1] + 8 * j - 24, :])
        out[me_dp ^ j] = rows


def finish(hcol, n_early, late, came, *refs):
    early = refs[:n_early]
    finish_outs(hcol, late, came, early, *refs[n_early:])


def finish_outs(hcol, late, came, early, gains, shifts, branch, qv, up, tl_in, tl_out, b1, b2, *refs_held):
    if len(early) == 1:
        v = late[...] + came[...]
    else:
        v = get_halves(late, late.shape[0] - 32, 16) + get_halves(came, late.shape[0] - 32, 16)
    hidden = tl_in.shape[0]
    if len(early) == 1:
        total = early[0][...]
    else:
        me, n = position()[0], (early[0].shape[0] - 32) // 2
        held = refs_held[0]
        for i, ref in enumerate(early):
            for k in (0, 1):
                held[pl.ds(pl.multiple_of((me ^ (2 * i + k)) * n, 8), n), :] = ref[k * n : (k + 1) * n, :].astype(F32)
        total = held[...]
    tl_in[...] = total[0:hidden, :]
    tl_out[...] = total[hidden : hidden + 8, 0:hidden]
    rest = total[hidden + 8 : hidden + 16, :]
    b1[...] = rest[3:4, 0:hidden]
    b2[...] = rest[4:5, 0:8]
    gains[...] = jnp.concatenate([v[3:4, :], v[0:1, :], rest[0:1, :]], axis=0)
    shifts[...] = jnp.concatenate([v[4:5, :], v[1:2, :], rest[1:2, :]], axis=0)
    branch[...] = jnp.concatenate([v[2:3, :], rest[2:3, :]], axis=0)
    for m in range(4):
        qv[0:1, m * hcol : (m + 1) * hcol] = v[9 + m : 10 + m, 0:hcol]
        qv[1:2, m * hcol : (m + 1) * hcol] = v[9 + m : 10 + m, 256 : 256 + hcol]
        width = v.shape[1]
        up[0:1, m * width : (m + 1) * width] = v[5 + m : 6 + m, :]


def nbytes(a):
    return a.size * a.dtype.itemsize


def run(kernel, name, outs, ins, smem=0, scratch=(), flops=0, deps=(), smem_more=()):
    spaces = [pltpu.SMEM if i < smem or i in smem_more else pltpu.VMEM for i in range(len(ins) + len(deps))]
    held = sum(nbytes(a) for a in [*ins, *deps, *outs]) + sum(nbytes(s) for s in scratch)
    return pl.pallas_call(
        kernel,
        out_shape=tuple(outs),
        in_specs=[pl.BlockSpec(memory_space=space) for space in spaces],
        out_specs=tuple(pl.BlockSpec(memory_space=pltpu.VMEM) for _ in outs),
        scratch_shapes=[pltpu.VMEM(s.shape, s.dtype) for s in scratch],
        compiler_params=pltpu.CompilerParams(
            vmem_limit_bytes=int(1.25 * held) + 6 * 1024 * 1024 if split_axis() else 56 * 1024 * 1024
        ),
        cost_estimate=pl.CostEstimate(flops=int(1.15e9 * COST.get(name, 1.0)), bytes_accessed=1024, transcendentals=0),
        name=name,
    )(*ins, *deps)


def struct(*shape, dtype=BF16):
    return jax.ShapeDtypeStruct(shape, dtype)


def local(
    tokens, w_qkv, w_out, w_up, w_down, norm_gains, norm_shifts, branch_bias, qv_bias, up_bias,
    tl_in, tl_bias1, tl_out, tl_bias2, keep_mask, assign, cotangent,
):
    clips, frames, patch_dev, D = tokens.shape
    half = clips // 2
    G = GROUP
    n_batch = half // G
    R = G * 96
    hcol = w_qkv.shape[1]
    heads = hcol // HD
    hid = w_up.shape[0]
    tlh = tl_in.shape[0]
    n_mp = lax.axis_size("mp")
    grid = split_axis()
    known = {}

    def waits(name, b=0):
        return [known[item] for item in WAITS.get(name, ()) if item in known] if b == 0 else []

    def gather_dp(values, steps, name=""):
        if not grid:
            return [lax.all_gather(values, "dp", axis=0, tiled=True)], [(0,)], [], []
        if steps == 1:
            along = [swap(values, "dp", 2 * k) for k in (1, 2, 3)]
            across = [swap(item, "dp", 1) for item in [values, *along]]
            return [values, *along, *across], [(0,), (2,), (4,), (6,), (1,), (3,), (5,), (7,)], along, across
        second = swap(values, "dp", 4)
        near = joined([values, second], waits("join_" + name))
        far = swap(near, "dp", 2)
        if steps == 3:
            return [near, far, swap(joined([second, far], waits("rest_" + name)), "dp", 1)], [(0, 4), (2, 6), (5, 3, 7)], None, None
        across = [swap(near, "dp", 1), swap(far, "dp", 1)]
        return [near, far, *across], [(0, 4), (2, 6), (1, 5), (3, 7)], [far], across

    def joined(group, deps=()):
        if len(group) == 1:
            return group[0]
        rows, width = sum(item.shape[0] for item in group), group[0].shape[1]
        out = struct(rows, width, dtype=group[0].dtype)
        return run(functools.partial(join, len(group)), "join", [out], group, deps=deps)[0]

    def after(value, deps):
        return run(gate, "gate", [struct(*value.shape)], [value], deps=deps)[0] if deps else value

    def pair(part, sent, deps=()):
        mine = run(chip_sum, "chip_sum", [struct(R, D)], [part, swap(sent, "mp", 1)], deps=deps)[0]
        return mine, swap(mine, "mp", 2)

    flat = tokens.reshape(clips * patch_dev, D)
    steps = 3 if OWN_FIRST and grid else 2
    if steps == 3:
        across = swap(joined([w_up.T, w_down.T], waits("own")), "dp", 1)
        known.update(own_x=across)
    wa = run(turn, "turn", [struct(w_out.shape[1], 4 * hcol)], [w_qkv.reshape(3 * hcol, -1), w_out])[0]
    far = swap(flat, "mp", 2)
    xs = [flat, swap(flat, "mp", 1), far, swap(far, "mp", 1)]
    wa_parts, wa_order, _, _ = gather_dp(wa, P1_STEPS, "wa")
    known.update(zip(("wa_n", "wa_z", "wa_x0", "wa_x1") if P1_STEPS == 2 else ("wa_n", "wa_z1", "wa_z2", "wa_z3"), wa_parts))
    up_parts, up_order, _, _ = gather_dp(after(w_up.T, waits("gate_up")), steps, "up")
    known.update(zip(("up_n", "up_z", "up_x0", "up_x1"), up_parts))
    down_parts, down_order, _, _ = gather_dp(after(w_down.T, waits("gate_down")), steps, "down")
    known.update(zip(("down_n", "down_z", "down_x0", "down_x1"), down_parts))
    if steps == 3:
        up_parts, up_order = [*up_parts, across], [*up_order, (1, None)]
        down_parts, down_order = [*down_parts, across], [*down_order, (None, 1)]

    if grid:
        blocks = struct(4, 8, D)
        cot_far, cot_near = run(cot_first, "cot_first", [blocks] * 2, [cotangent[0]], deps=waits("cot_first"))
        cot_came = swap(cot_far, "dp", 1)
        cot_go, cot_stay = run(pair_first, "pair_first", [blocks] * 2, [cot_near, cot_came])
        cot_one = swap(cot_go, "dp", 2)
        cot_go = run(pair_second, "pair_second", [blocks], [cot_stay, cot_one])[0]
        cots = [cot_stay, cot_one, swap(cot_go, "dp", 4)]
    else:
        cots = [lax.all_to_all(cotangent, "dp", split_axis=1, concat_axis=0, tiled=True)[:, 0]]
    per_row = 2 * R * D

    early = None
    n_vec = tlh + 64
    kept = []
    wa_all = wf_all = None
    for b in range(n_batch):
        first = b == 0
        x_other, x_own, n_other, n_own = run(
            functools.partial(prep, (G, half, b)), "prep", [struct(R, D)] * 4, [*xs, norm_gains, norm_shifts],
            scratch=[struct(2 * G, 4, 24, D, dtype=F32)], deps=waits("prep", b),
        )

        def attention(side, n1, deps):
            nonlocal wa_all
            fresh = wa_all is None
            weights = wa_parts if fresh else [wa_all]
            outs = [struct(R, hcol)] * 4 + [struct(G * heads * 96, 96), struct(R, D, dtype=F32 if side else BF16)]
            found = run(
                functools.partial(attn_fwd, (G, half, b, side, wa_order if fresh else None, len(deps))),
                "attn_fwd_own" if side else "attn_fwd_other", outs + ([struct(D, 4 * hcol)] if fresh else []),
                [n1, keep_mask, qv_bias, *weights], flops=per_row * 4 * hcol, deps=deps,
            )
            if fresh:
                wa_all = found[6]
            return found[:6]

        a_other = attention(0, n_other, waits("attn_fwd_other", b))
        a_own = attention(1, n_own, waits("attn_fwd_own", b))
        mine, came = pair(a_own[5], a_other[5], waits("chip_sum_0", b))
        res, n2 = run(
            mid_norm, "mid_norm", [struct(R, D, dtype=F32), struct(R, D)],
            [mine, came, x_own, branch_bias, norm_gains, norm_shifts], deps=waits("mid_norm", b),
        )
        n2_other = swap(n2, "mp", 1)

        def ffn(side, rows):
            nonlocal wf_all
            fresh = wf_all is None
            weights = [*up_parts, *down_parts] if fresh else wf_all
            outs = [struct(R, hid)] * 2 + [struct(R, D, dtype=F32 if side else BF16)]
            found = run(
                functools.partial(ffn_fwd, (up_order, down_order) if fresh else None),
                "ffn_fwd_own" if side else "ffn_fwd_other", outs + ([struct(D, hid)] * 2 if fresh else []),
                [rows, up_bias[None, :], *weights], flops=per_row * 2 * hid,
            )
            if fresh:
                wf_all = found[3:]
            return found[:3]

        f_own = ffn(1, n2)
        f_other = ffn(0, n2_other)
        mine, came = pair(f_own[2], f_other[2])
        grad_block, grad_block_low, vec = run(
            functools.partial(learner, (G, half, b, len(cots), grid)), "learner",
            [struct(R, D, dtype=F32), struct(R + 8 * G + (2 * n_vec if grid else 0), D), struct(n_vec, D, dtype=F32)],
            [assign, res, mine, came, branch_bias, norm_gains, norm_shifts, tl_in, tl_bias1[None, :], tl_out,
             tl_bias2[None, :], keep_mask, *cots], smem=1, scratch=[struct(8, 8, D)] if grid else [], flops=per_row * tlh,
        )
        early = vec if first else early + vec
        kept.append((x_other, x_own, n_other, n_own, a_other, a_own, res, n2, n2_other, f_own, f_other, grad_block, grad_block_low))

    def grads(name, groups, widths, cuts, extra=None, more=(), more_outs=(), ride=(), smem_more=(), deps=()):
        lefts, rights, terms = [], [], []
        for pairs in groups:
            mine = []
            for left, right in pairs:
                found = [i for i, known in enumerate(lefts) if known is left]
                if not found:
                    lefts.append(left)
                    found = [len(lefts) - 1]
                rights.append(right)
                mine.append((found[0], len(rights) - 1))
            terms.append(mine)
        width = sum(widths)
        outs = [struct(D, width, dtype=F32)]
        if grid:
            outs = [item for (cut, _), more_rows in zip(cuts, ride or (0,) * len(cuts))
                    for item in (struct(D // 2 + more_rows, cut), struct(D // 2, cut, dtype=F32))]
        base = len(lefts) + len(rights)
        return run(
            functools.partial(weight_grads, (len(lefts), len(rights), widths, terms, cuts if grid else (), extra,
                                             len(more), len(deps))),
            name, outs + list(more_outs), [*lefts, *rights, *more], deps=deps,
            scratch=[struct(D, width, dtype=F32)], flops=n_batch * 2 * per_row * width,
            smem_more=[base + i for i in smem_more],
        )

    def to_owner(order, send, own, rides=(), deps=()):
        size, width = own.shape[0] // 4, own.shape[1]
        ride = 32 + n_vec // 2 if rides else 0
        outs = [struct(2 * size + ride, width), struct(2 * size, width, dtype=F32)]
        outs += [struct(32, width), struct(n_vec // 2, width)] if rides else []
        return run(functools.partial(owner_first, ride), "owner_first", outs, [swap(send, "dp", order[0]), own, *rides], deps=deps)

    def to_last(order, first, deps=()):
        go, own = first[0:2]
        size, width = own.shape[0] // 2, own.shape[1]
        ride = go.shape[0] - 2 * size
        came = swap(go, "dp", order[1])
        outs = [struct(size + (32 + n_vec // 4 if ride else 0), width), struct(size, width, dtype=F32)]
        outs += [struct(n_vec // 4, width)] if ride else []
        go, own, *early = run(functools.partial(owner_second, ride), "owner_second", outs, [came, own, *first[2:]], deps=deps)
        return [own, swap(go, "dp", order[2]), came, *early]

    def turned(sums, heights):
        return run(functools.partial(turned_sum, len(sums)), "turned_sum",
                   [struct(n, sums[0][0].shape[0], dtype=F32) for n in heights], [t for item in sums for t in item[0:2]])

    def last_sum(item, deps=()):
        return run(add_last, "add_last", [struct(*item[0].shape, dtype=F32)], item[0:2], deps=deps)[0].T

    wu, wd = wf_all
    later = []
    sides = range(n_batch)
    halves = []
    for b in sides:
        f_own, f_other, low = kept[b][9], kept[b][10], kept[b][12]
        block_other = swap(low, "mp", 1)
        back_outs = [struct(R, hid), struct(1, hid, dtype=F32)]
        part_own, g_pre_own, up_sum = run(
            functools.partial(ffn_bwd, 0), "ffn_bwd_own", [struct(R, D, dtype=F32)] + back_outs,
            [low, f_own[1], wu, wd], flops=per_row * 2 * hid,
        )
        part_other, g_pre_other, up_sum = run(
            functools.partial(ffn_bwd, 1), "ffn_bwd_other", [struct(R, D)] + back_outs,
            [block_other, f_other[1], wu, wd, up_sum], flops=per_row * 2 * hid,
        )
        halves.append((block_other, g_pre_own, g_pre_other, up_sum, part_own, part_other))

    down_pairs = [p for b in sides for p in ((kept[b][12], kept[b][9][0]), (halves[b][0], kept[b][10][0]))]
    up_pairs = [p for b in sides for p in ((kept[b][7], halves[b][1]), (kept[b][8], halves[b][2]))]
    if grid:
        down_send, down_own, pool_kept, early = grads(
            "down_grads", [down_pairs], (hid,), ((hid, DOWN),), extra=functools.partial(ride_down, half, R, G),
            more=(assign, kept[0][12], halves[0][0]), more_outs=[struct(64, D, dtype=F32), struct(n_vec // 2, D)],
            ride=(32 + n_vec // 2,), smem_more=(0,),
        )
        up_send, up_own = grads("up_grads", [up_pairs], (hid,), ((hid, ORDER["up"]),))
        known.update(down_send=down_send, up_send=up_send)
        down_sums = to_owner(DOWN, down_send, down_own, (pool_kept, early), waits("down_first"))
        known.update(down_first=down_sums[1])
    else:
        down_sums = grads("down_grads", [down_pairs], (hid,), ())
        up_sums = grads("up_grads", [up_pairs], (hid,), ())
        early = lax.psum(early + swap(early, "mp", 1), "dp")

    for b in sides:
        x_other, x_own, n_other, n_own, a_other, a_own, res = kept[b][:7]
        grad_block = kept[b][11]
        block_other, g_pre_own, g_pre_other, up_sum, part_own, part_other = halves[b]
        mine, came = pair(part_own, part_other, waits("chip_sum_2", b))
        grad_res, grad_res_low, mid_vec = run(
            mid_back, "mid_back", [struct(R, D, dtype=F32), struct(R, D), struct(8, D, dtype=F32)],
            [mine, came, res, grad_block, norm_gains], deps=waits("mid_back", b),
        )
        res_other = swap(grad_res_low, "mp", 1)
        deps = waits("attn_bwd", b)
        found = run(
            functools.partial(attn_bwd, len(deps)), "attn_bwd", [struct(R, hcol)] * 6,
            [grad_res_low, res_other, *a_own[:3], a_own[4], *a_other[:3], a_other[4], wa_all],
            scratch=[struct(R, hcol)], deps=deps,
        )
        later.append((res_other, grad_res_low, found[0:3], found[3:6], grad_res, mid_vec, up_sum))
    if grid:
        known.update(late=later[0][2][0])
    mid_total = sum([later[b][5] for b in sides[1:]], later[0][5])
    up_total = sum([later[b][6] for b in sides[1:]], later[0][6])
    *found, late = grads(
        "attn_grads",
        [[p for b in sides for p in ((kept[b][3], later[b][2][w]), (kept[b][2], later[b][3][w]))] for w in range(3)]
        + [[p for b in sides for p in ((later[b][1], kept[b][5][3]), (later[b][0], kept[b][4][3]))]],
        (hcol,) * 4, ((2 * hcol, ORDER["first"]), (2 * hcol, ORDER["second"])), deps=waits("attn_grads"),
        extra=late_vectors, more=(wa_all, norm_gains, norm_shifts, mid_total, up_total), ride=(64, 0) if grid else (),
        more_outs=([struct(64, 2 * hcol)] if grid else []) + [struct(16, D, dtype=F32)],
    )
    if grid:
        known.update(attn_send=found[0])
        halves_first = {}
        size, width = D // 8, 2 * hcol
        for c, name in enumerate(("first", "second")):
            if c:
                halves_first[name] = to_owner(ORDER[name], *found[2 * c : 2 * c + 2], deps=waits(name + "_first"))
            else:
                halves_first[name] = run(
                    late_first, "late_first", [struct(2 * size + 64, width), struct(2 * size, width, dtype=F32), struct(64, width)],
                    [swap(found[0], "dp", ORDER[name][0]), found[1], found[4]], deps=waits(name + "_first"),
                )
            known[name + "_first"] = halves_first[name][1]
        down_z = to_last(DOWN, down_sums, waits("down_second"))
        known.update(down_z2=down_z[1], down_second=down_z[0])
        up_sums = to_owner(ORDER["up"], up_send, up_own, deps=waits("up_first"))
        known.update(up_first=up_sums[1])
        up_z = to_last(ORDER["up"], up_sums, waits("up_second"))
        known.update(up_second=up_z[0], up_z2=up_z[1])
        halves_last = {}
        for name in ("first", "second"):
            if name == "first":
                go, own, late_own = halves_first[name]
                go, own, late_own = run(
                    late_second, "late_second", [struct(size + 32, width), struct(size, width, dtype=F32), struct(32, width)],
                    [swap(go, "dp", ORDER[name][1]), own, late_own], deps=waits("first_second"),
                )
                halves_last[name] = [own, swap(go, "dp", ORDER[name][2]), late_own]
            else:
                halves_last[name] = to_last(ORDER[name], halves_first[name], waits(name + "_second"))
            known[name + "_second"] = halves_last[name][0]

    toks = []
    for b in sides:
        x_other, x_own = kept[b][:2]
        g_own, g_other, grad_res = later[b][2:5]
        rows = 2 * G * 24
        deps = waits("token_bwd", b)
        near_other, near_own, far_both = run(
            functools.partial(token_bwd, (G, len(deps))), "token_bwd", [struct(rows, D, dtype=F32)] * 2 + [struct(2 * rows, D)],
            [*g_own, x_own, *g_other, x_other, wa_all, norm_gains, grad_res],
            scratch=[struct(G, 4, 24, D, dtype=F32), struct(R, D, dtype=F32)], deps=deps,
        )
        tok_own, tok_far = run(
            token_sum, "token_sum", [struct(rows, D, dtype=F32), struct(rows, D)],
            [near_other, near_own, swap(far_both, "mp", 1)], deps=waits("token_sum", b),
        )
        grad_tok = run(add_last, "token_last", [struct(rows, D, dtype=F32)], [tok_own, swap(tok_far, "mp", 2)], deps=waits("token_last", b))[0]
        toks.append(grad_tok.reshape(2, G, 1, patch_dev, D))
    grad_tokens = jnp.stack(toks, axis=1).reshape(clips, 1, patch_dev, D)

    if grid:
        both = run(early_sum, "early_sum", [struct(n_vec // 4 + 16, D, dtype=F32)],
                   [down_z[3], down_z[1], halves_last["first"][2], halves_last["first"][1]], deps=waits("early_sum"))[0]
        late = run(fold, "fold", [struct(n_vec // 2 + 32, D)], [both, swap(both, "mp", 1)], deps=waits("fold"))[0]
        late_came = swap(late, "mp", 2)
        early = [late, late_came]
    else:
        late = late + swap(late, "mp", 1)
        late = lax.psum(late + swap(late, "mp", 2), "dp")
        late_came = jnp.zeros_like(late)
        early = [early]
    gains, shifts, branch, grad_qv, grad_upbias, grad_tl_in, grad_tl_out, grad_b1, grad_b2 = run(
        functools.partial(finish, hcol, len(early)), "finish",
        [struct(3, D, dtype=F32), struct(3, D, dtype=F32), struct(2, D, dtype=F32), struct(2, D, dtype=F32),
         struct(1, n_mp * hid, dtype=F32), struct(tlh, D, dtype=F32), struct(8, tlh, dtype=F32), struct(1, tlh, dtype=F32),
         struct(1, 8, dtype=F32)], [late, late_came, *early],
        scratch=[struct(n_vec, D, dtype=F32)] if grid else [],
    )

    if grid:
        grad_down = last_sum(down_z, waits("down_last"))
        pooled_out = run(functools.partial(pool_last, (D // 4, D // 8)), "pool_last", [struct(8, 8, D)],
                         [down_sums[2], down_z[2], down_z[1]], deps=waits("pool_last"))[0][None]
        grad_up = last_sum(up_z, waits("up_last"))
        grad_qkv, grad_out = turned(
            [halves_last["first"], halves_last["second"]],
            [3 * hcol, hcol],
        )
    else:
        grad_down, grad_up, attn = [
            lax.psum_scatter(item, "dp", scatter_dimension=0, tiled=True).T for item in (down_sums[0], up_sums[0], found[0])
        ]
        grad_qkv, grad_out = attn[: 3 * hcol], attn[3 * hcol :]
        both = jnp.stack([jnp.concatenate([halves[b][0][R:], kept[b][12][R:]], axis=0).reshape(2, G, 8, D) for b in sides], axis=1)
        both = both.reshape(clips, 8, D)
        places = (assign + half * (1 - (lax.axis_index("mp") & 1))) % clips
        table = (places[:, None] == lax.iota(jnp.int32, clips)[None, :]).astype(BF16)
        permuted = jnp.einsum("sc,ckd->skd", table, both, preferred_element_type=F32).astype(BF16)
        pooled_out = lax.all_to_all(permuted[:, None], "dp", split_axis=0, concat_axis=1, tiled=True)
    return (
        pooled_out,
        grad_tokens,
        grad_qkv.reshape(3, hcol, -1),
        grad_out,
        grad_up,
        grad_down,
        gains,
        shifts,
        branch,
        grad_qv,
        grad_upbias[0],
        grad_tl_in,
        grad_b1[0],
        grad_tl_out,
        grad_b2[0],
    )


def solution(mesh):
    in_specs = (
        P(None, "dp", "mp", None),
        P(None, "mp", "dp"),
        P("mp", "dp"),
        P("mp", "dp"),
        P("mp", "dp"),
        P(),
        P(),
        P(),
        P(),
        P(),
        P(),
        P(),
        P(),
        P(),
        P(),
        P(),
        P("dp", None, None, None),
    )
    out_specs = (
        P("dp", None, None, None),
        P(None, "dp", "mp", None),
        P(None, "mp", "dp"),
        P("mp", "dp"),
        P("mp", "dp"),
        P("mp", "dp"),
        P(),
        P(),
        P(),
        P(),
        P(),
        P(),
        P(),
        P(),
        P(),
    )
    return jax.shard_map(local, mesh=mesh, in_specs=in_specs, out_specs=out_specs, check_vma=False)
```

time: 701 us -> 158 us (0.23); the launches traced: 692 us -> 158 us
  waiting for transfers between devices: 361 us -> 63.8 us
  blocking collectives: 173 us -> 0 us
  matrix products: 56.8 us -> 0 us
  local copies, waits for them, and re-layouts: 53 us -> 1.78 us
  starting transfers between devices: 9.92 us -> 51.7 us
  Pallas kernels: 0 us -> 39.5 us
  other arithmetic: 19.9 us -> 0 us
  between operations: 18.3 us -> 1.1 us
    reduce_scatter x6 -> x0, waiting for transfers between devices: 208 us -> none  [the longest x1 72.3 us: local(): lax.psum_scatter(weight_acc[3], 'dp', scatter_dimension=1, tiled=True)]
    all_gather x10 -> x0, blocking collectives: 131 us -> none  [the longest x1 39.1 us: local(): lax.all_gather(w_qkv, 'dp', axis=2, tiled=True)]
    unnamed x22 -> x0, waiting for transfers between devices: 113 us -> none
    ppermute x0 -> x42, waiting for transfers between devices: none -> 63.8 us  [swap(): return lax.ppermute(values, axis, [(i, i ^ bit) for i in range(size)])]
    dot_general x56 -> x0, matrix products: 56.8 us -> none  [matmul(): return jnp.einsum(form, left, right, preferred_element_type=jnp.float32)]
    ppermute x0 -> x42, starting transfers between devices: none -> 51.7 us  [swap(): return lax.ppermute(values, axis, [(i, i ^ bit) for i in range(size)])]
    psum x1 -> x0, blocking collectives: 41.8 us -> none  [local(): vector_sums = lax.psum(vector_acc, ('dp', 'mp'))]
    pallas_call x0 -> x47, Pallas kernels: none -> 39.5 us  [run(): pl.pallas_call(kernel, out_shape=tuple(outs), in_specs=[pl.BlockSpec(memo...]
  transfers between devices with their start and end apart: 18 -> 42, of which waited for: 14 -> 18; matrix products, arithmetic and copies ran while one was open for 13% -> 0% of each run, Pallas kernels for 0% -> 20%
where the time goes in v1:
time: 158 us
  waiting for transfers between devices  63.8 us (40%)
  starting transfers between devices  51.7 us (33%)
  Pallas kernels  39.5 us (25%)
  local copies, waits for them, and re-layouts  1.78 us (1%)
    ppermute x42, waiting for transfers between devices, swap(): return lax.ppermute(values, axis, [(i, i ^ bit) for i in range(size)])  63.8 us
    ppermute x42, starting transfers between devices, swap(): return lax.ppermute(values, axis, [(i, i ^ bit) for i in range(size)])  51.7 us
    pallas_call x47, Pallas kernels, run(): pl.pallas_call(kernel, out_shape=tuple(outs), in_specs=[pl.BlockSpec(memo...  39.5 us
  transfers between devices with their start and end apart: 42, of which 18 were waited for; matrix products, arithmetic and copies ran while one was open for 0% of the time, Pallas kernels for 20%

profile of v1, /device:TPU:0, one launch (start us, length us, event | category | flops | bytes accessed | tf_op | source)
XLA Modules:
  0.0 157.8 jit_solution(17812451913638402680)
XLA Ops:
  2.5 4.1 %collective-permute-start.3 = (bf16[96,768]{1,0:T(8,128)(2,1)S(1)}, bf16[96,768]{1,0:T(8,128)(2,1)S(1)}, u32[]{:S(2)}, u32[]{:S(2)}) collective-permute-start(bf16[96,768]{1,0:T(8,128)(2,1)S(1)} %turn.1.refs_0_), channel_id=1, source_target_pairs={{0,16},{4,20},{8,24},{12,28},{16,0},{20,4},{24,8},{28,12},{1,17},{... | collective-permute-start | bytes 442376 | tf_op jit(solution)/shard_map/ppermute | solution.py:48
  6.6 1.6 collective-permute-start.7
  8.2 1.5 collective-permute-start.1
  9.7 3.9 %collective-permute-done.3.refs_1_ = bf16[96,768]{1,0:T(8,128)(2,1)S(1)} collective-permute-done((bf16[96,768]{1,0:T(8,128)(2,1)S(1)}, bf16[96,768]{1,0:T(8,128)(2,1)S(1)}, u32[]{:S(2)}, u32[]{:S(2)}) %collective-permute-start.3) | collective-permute-done | bytes 147488 | tf_op jit(solution)/shard_map/ppermute | solution.py:48
  14.4 1.5 collective-permute-start.5
  15.9 3.4 %collective-permute-start.8 = (bf16[96,768]{1,0:T(8,128)(2,1)S(1)}, bf16[96,768]{1,0:T(8,128)(2,1)S(1)}, u32[]{:S(2)}, u32[]{:S(2)}) collective-permute-start(bf16[96,768]{1,0:T(8,128)(2,1)S(1)} %gate.2.refs_0_), channel_id=1, source_target_pairs={{0,16},{4,20},{8,24},{12,28},{16,0},{20,4},{24,8},{28,12},{1,17},{... | collective-permute-start | bytes 442376 | tf_op jit(solution)/shard_map/ppermute | solution.py:48
  19.9 5.2 %collective-permute-done.4.refs_3_.refs_4_ = bf16[192,768]{1,0:T(8,128)(2,1)S(1)} collective-permute-done((bf16[192,768]{1,0:T(8,128)(2,1)S(1)}, bf16[192,768]{1,0:T(8,128)(2,1)S(1)}, u32[]{:S(2)}, u32[]{:S(2)}) %collective-permute-start.4) | collective-permute-done | bytes 294944 | tf_op jit(solution)/shard_map/ppermute | solution.py:48
  25.0 1.2 collective-permute-start.6
  26.3 1.9 %collective-permute-start.9 = (bf16[192,768]{1,0:T(8,128)(2,1)S(1)}, bf16[192,768]{1,0:T(8,128)(2,1)S(1)}, u32[]{:S(2)}, u32[]{:S(2)}) collective-permute-start(bf16[192,768]{1,0:T(8,128)(2,1)S(1)} %join.8.refs_7_.rest_0_.refs_2_), channel_id=1, source_target_pairs={{0,8},{4,12},{8,0},{12,4},{16,24},{20,28},{24,16},{28,20},{1,9},{5... | collective-permute-start | bytes 884744 | tf_op jit(solution)/shard_map/ppermute | solution.py:48
  28.3 3.3 %collective-permute-start.10 = (bf16[96,768]{1,0:T(8,128)(2,1)S(1)}, bf16[96,768]{1,0:T(8,128)(2,1)S(1)}, u32[]{:S(2)}, u32[]{:S(2)}) collective-permute-start(bf16[96,768]{1,0:T(8,128)(2,1)S(1)} %gate.3.refs_0_), channel_id=1, source_target_pairs={{0,16},{4,20},{8,24},{12,28},{16,0},{20,4},{24,8},{28,12},{1,17},{... | collective-permute-start | bytes 442376 | tf_op jit(solution)/shard_map/ppermute | solution.py:48
  31.6 1.9 %prep.1 = (bf16[384,768]{1,0:T(8,128)(2,1)S(1)}, bf16[384,768]{1,0:T(8,128)(2,1)S(1)}, bf16[384,768]{1,0:T(8,128)(2,1)S(1)}, bf16[384,768]{1,0:T(8,128)(2,1)S(1)}) custom-call(bf16[192,768]{1,0:T(8,128)(2,1)S(1)} %bitcast.20, bf16[192,768]{1,0:T(8,128)(2,1)S(1)} %collective-permute-done.refs_1_, bf16[192,768]{1,0:T(8,128)(2,1)S(1)} %collective-permute-done.1.refs_2_, ...), custom_call_target="tpu_custom_call" | custom-call | flops 345000000 | bytes 1024 | tf_op jit(solution)/shard_map/prep/pallas_call | solution.py:702
  33.6 1.9 %attn_fwd_other.1 = (bf16[384,192]{1,0:T(8,128)(2,1)S(1)}, bf16[384,192]{1,0:T(8,128)(2,1)S(1)}, bf16[384,192]{1,0:T(8,128)(2,1)S(1)}, bf16[384,192]{1,0:T(8,128...) custom-call(bf16[384,768]{1,0:T(8,128)(2,1)S(1)} %get-tuple-element.112.refs_0_, ...), custom_call_target="tpu_custom_call" | custom-call | flops 2300000000 | bytes 1024 | tf_op jit(solution)/shard_map/attn_fwd_other/pallas_call | solution.py:702
  35.6 1.7 %collective-permute-done.10.refs_1_.refs_0_ = bf16[96,768]{1,0:T(8,128)(2,1)S(1)} collective-permute-done((bf16[96,768]{1,0:T(8,128)(2,1)S(1)}, bf16[96,768]{1,0:T(8,128)(2,1)S(1)}, u32[]{:S(2)}, u32[]{:S(2)}) %collective-permute-start.10) | collective-permute-done | bytes 147488 | tf_op jit(solution)/shard_map/ppermute | solution.py:48
  37.4 3.4 %collective-permute-start.14 = (bf16[192,768]{1,0:T(8,128)(2,1)S(1)}, bf16[192,768]{1,0:T(8,128)(2,1)S(1)}, u32[]{:S(2)}, u32[]{:S(2)}) collective-permute-start(bf16[192,768]{1,0:T(8,128)(2,1)S(1)} %join.9.refs_5_.rest_0_.refs_6_), channel_id=1, source_target_pairs={{0,8},{4,12},{8,0},{12,4},{16,24},{20,28},{24,16},{28,20},{1,9},{5... | collective-permute-start | bytes 884744 | tf_op jit(solution)/shard_map/ppermute | solution.py:48
  41.4 1.9 %attn_fwd_own.1 = (bf16[384,192]{1,0:T(8,128)(2,1)S(1)}, bf16[384,192]{1,0:T(8,128)(2,1)S(1)}, bf16[384,192]{1,0:T(8,128)(2,1)S(1)}, bf16[384,192]{1,0:T(8,128)(...) custom-call(bf16[384,768]{1,0:T(8,128)(2,1)S(1)} %get-tuple-element.111.refs_0_, s32[8,96]{1,0:T(8,128)S(1)} %copy-done.12, ...), custom_call_target="tpu_custom_call" | custom-call | flops 4600000000 | bytes 1024 | tf_op jit(solution)/shard_map/attn_fwd_own/pallas_call | solution.py:702
  43.4 1.6 %collective-permute-start.12 = (bf16[384,768]{1,0:T(8,128)(2,1)S(1)}, bf16[384,768]{1,0:T(8,128)(2,1)S(1)}, u32[]{:S(2)}, u32[]{:S(2)}) collective-permute-start(bf16[384,768]{1,0:T(8,128)(2,1)S(1)} %chip_sum.3.mine), channel_id=1, source_target_pairs={{0,2},{1,3},{2,0},{3,1},{4,6},{5,7},{6,4},{7,5},{8,10},{9,11},{10,... | collective-permute-start | bytes 1769480 | tf_op jit(solution)/shard_map/ppermute | solution.py:48
  46.6 9.4 %collective-permute-done.12.came = bf16[384,768]{1,0:T(8,128)(2,1)S(1)} collective-permute-done((bf16[384,768]{1,0:T(8,128)(2,1)S(1)}, bf16[384,768]{1,0:T(8,128)(2,1)S(1)}, u32[]{:S(2)}, u32[]{:S(2)}) %collective-permute-start.12) | collective-permute-done | bytes 589856 | tf_op jit(solution)/shard_map/ppermute | solution.py:48
  56.7 3.5 %collective-permute-done.15.refs_8_ = bf16[288,768]{1,0:T(8,128)(2,1)S(1)} collective-permute-done((bf16[288,768]{1,0:T(8,128)(2,1)S(1)}, bf16[288,768]{1,0:T(8,128)(2,1)S(1)}, u32[]{:S(2)}, u32[]{:S(2)}) %collective-permute-start.15) | collective-permute-done | bytes 442400 | tf_op jit(solution)/shard_map/ppermute | solution.py:48
  60.1 2.1 %ffn_fwd_own.1 = (bf16[384,768]{1,0:T(8,128)(2,1)S(1)}, bf16[384,768]{1,0:T(8,128)(2,1)S(1)}, f32[384,768]{1,0:T(8,128)S(1)}, bf16[768,768]{1,0:T(8,128)(2,1)S(1)}, bf16[768,768]{1,0:T(8,128)(2,1)S(1)}) custom-call(bf16[384,768]{1,0:T(8,128)(2,1)S(1)} %get-tuple-element.118.refs_0_, f32[1,3072]{1,0:T(1,128)S(1)} %bitcast.27, ...), custom_call_target="tpu_custom_call" | custom-call | flops 9200000000 | bytes 1024 | tf_op jit(solution)/shard_map/ffn_fwd_own/pallas_call | solution.py:702
  62.3 2.0 %ffn_fwd_other.1 = (bf16[384,768]{1,0:T(8,128)(2,1)S(1)}, bf16[384,768]{1,0:T(8,128)(2,1)S(1)}, bf16[384,768]{1,0:T(8,128)(2,1)S(1)}) custom-call(bf16[384,768]{1,0:T(8,128)(2,1)S(1)} %collective-permute-done.16.refs_0_.refs_1_, f32[1,3072]{1,0:T(1,128)S(1)} %bitcast.28, bf16[768,768]{1,0:T(8,128)(2,1)S(1)} %get-tuple-element.120.refs_2_.wu, ...), custom_call_target="tpu_custom_call" | custom-call | flops 4600000000 | bytes 1024 | tf_op jit(solution)/shard_map/ffn_fwd_other/pallas_call | solution.py:702
  64.4 2.0 %collective-permute-done.17.came = bf16[384,768]{1,0:T(8,128)(2,1)S(1)} collective-permute-done((bf16[384,768]{1,0:T(8,128)(2,1)S(1)}, bf16[384,768]{1,0:T(8,128)(2,1)S(1)}, u32[]{:S(2)}, u32[]{:S(2)}) %collective-permute-start.17) | collective-permute-done | bytes 589856 | tf_op jit(solution)/shard_map/ppermute | solution.py:48
  66.5 1.6 %collective-permute-start.18 = (bf16[384,768]{1,0:T(8,128)(2,1)S(1)}, bf16[384,768]{1,0:T(8,128)(2,1)S(1)}, u32[]{:S(2)}, u32[]{:S(2)}) collective-permute-start(bf16[384,768]{1,0:T(8,128)(2,1)S(1)} %chip_sum.4.refs_1_), channel_id=1, source_target_pairs={{0,2},{1,3},{2,0},{3,1},{4,6},{5,7},{6,4},{7,5},{8,10},{9,11},{10,... | collective-permute-start | bytes 1769480 | tf_op jit(solution)/shard_map/ppermute | solution.py:48
  68.6 3.7 %collective-permute-done.19.came = bf16[4,8,768]{2,1,0:T(8,128)(2,1)S(1)} collective-permute-done((bf16[4,8,768]{2,1,0:T(8,128)(2,1)S(1)}, bf16[4,8,768]{2,1,0:T(8,128)(2,1)S(1)}, u32[]{:S(2)}, u32[]{:S(2)}) %collective-permute-start.19) | collective-permute-done | bytes 49184 | tf_op jit(solution)/shard_map/ppermute | solution.py:48
  72.7 3.8 %collective-permute-done.20.came.refs_12_ = bf16[4,8,768]{2,1,0:T(8,128)(2,1)S(1)} collective-permute-done((bf16[4,8,768]{2,1,0:T(8,128)(2,1)S(1)}, bf16[4,8,768]{2,1,0:T(8,128)(2,1)S(1)}, u32[]{:S(2)}, u32[]{:S(2)}) %collective-permute-start.20) | collective-permute-done | bytes 49184 | tf_op jit(solution)/shard_map/ppermute | solution.py:48
  76.5 1.8 %collective-permute-start.21 = (bf16[4,8,768]{2,1,0:T(8,128)(2,1)S(1)}, bf16[4,8,768]{2,1,0:T(8,128)(2,1)S(1)}, u32[]{:S(2)}, u32[]{:S(2)}) collective-permute-start(bf16[4,8,768]{2,1,0:T(8,128)(2,1)S(1)} %pair_second.1), channel_id=1, source_target_pairs={{0,16},{4,20},{8,24},{12,28},{16,0},{20,4},{24,8},{28,12},{1,17},{... | collective-permute-start | bytes 147464 | tf_op jit(solution)/shard_map/ppermute | solution.py:48
  78.2 3.5 %collective-permute-done.21.refs_13_ = bf16[4,8,768]{2,1,0:T(8,128)(2,1)S(1)} collective-permute-done((bf16[4,8,768]{2,1,0:T(8,128)(2,1)S(1)}, bf16[4,8,768]{2,1,0:T(8,128)(2,1)S(1)}, u32[]{:S(2)}, u32[]{:S(2)}) %collective-permute-start.21) | collective-permute-done | bytes 49184 | tf_op jit(solution)/shard_map/ppermute | solution.py:48
  82.0 3.8 %learner.1 = (f32[384,768]{1,0:T(8,128)S(1)}, bf16[672,768]{1,0:T(8,128)(2,1)S(1)}, f32[128,768]{1,0:T(8,128)}) custom-call(s32[8]{0:T(128)S(1)} %copy-done.16, f32[384,768]{1,0:T(8,128)S(1)} %get-tuple-element.117.refs_0_.res, bf16[384,768]{1,0:T(8,128)(2,1)S(1)} %chip_sum.4.refs_1_, bf16[384,768]{1,0:T(8,128)(2,1)S(1)} %collective-permute-done.18.refs_2_, ...), custom_call_target="tpu_custom_call" | custom-call | flops 9200000000 | bytes 1024 | tf_op jit(solution)/shard_map/learner/pallas_call | solution.py:702
  85.8 1.2 ffn_bwd_own.1
  87.0 1.4 collective-permute-done.22.refs_1_.refs_6_.g
  88.4 1.2 ffn_bwd_other.1
  89.8 2.3 %down_grads.1 = (bf16[480,768]{1,0:T(8,128)(2,1)S(1)}, f32[384,768]{1,0:T(8,128)S(1)}, f32[64,768]{1,0:T(8,128)S(1)}, bf16[64,768]{1,0:T(8,128)(2,1)S(1)}) custom-call(bf16[672,768]{1,0:T(8,128)(2,1)S(1)} %get-tuple-element.127.refs_0_.refs_5_.g, bf16[672,768]{1,0:T(8,128)(2,1)S(1)} %collective-permute-done.22.refs_1_.refs_6_.g, ...), custom_call_target="tpu_custom_call" | custom-call | flops 4600000000 | bytes 1024 | tf_op jit(solution)/shard_map/down_grads/pallas_call | solution.py:702
  93.0 1.3 collective-permute-start.26
  94.3 1.6 up_grads.1
  96.3 12.1 %collective-permute-done.26.came = bf16[384,768]{1,0:T(8,128)(2,1)S(1)} collective-permute-done((bf16[384,768]{1,0:T(8,128)(2,1)S(1)}, bf16[384,768]{1,0:T(8,128)(2,1)S(1)}, u32[]{:S(2)}, u32[]{:S(2)}) %collective-permute-start.26) | collective-permute-done | bytes 589856 | tf_op jit(solution)/shard_map/ppermute | solution.py:48
  109.4 1.5 collective-permute-done.23.came
  111.7 2.7 %collective-permute-start.33 = (bf16[192,768]{1,0:T(8,128)(2,1)S(1)}, bf16[192,768]{1,0:T(8,128)(2,1)S(1)}, u32[]{:S(2)}, u32[]{:S(2)}) collective-permute-start(bf16[192,768]{1,0:T(8,128)(2,1)S(1)} %get-tuple-element.177), channel_id=1, source_target_pairs={{0,16},{4,20},{8,24},{12,28},{16,0},{20,4},{24,8},{28,12},{1,17},{... | collective-permute-start | bytes 884744 | tf_op jit(solution)/shard_map/ppermute | solution.py:48
  114.4 3.7 %attn_bwd.1 = (bf16[384,192]{1,0:T(8,128)(2,1)S(1)}, bf16[384,192]{1,0:T(8,128)(2,1)S(1)}, bf16[384,192]{1,0:T(8,128)(2,1)S(1)}, bf16[384,192]{1,0:T(8,128)(2,1)...) custom-call(bf16[384,768]{1,0:T(8,128)(2,1)S(1)} %get-tuple-element.147.g_own.refs_2_, ...), custom_call_target="tpu_custom_call" | custom-call | flops 18400000000 | bytes 1024 | tf_op jit(solution)/shard_map/attn_bwd/pallas_call | solution.py:702
  118.1 3.1 %attn_grads.1 = (bf16[448,384]{1,0:T(8,128)(2,1)S(1)}, f32[384,384]{1,0:T(8,128)S(1)}, bf16[384,384]{1,0:T(8,128)(2,1)S(1)}, f32[384,384]{1,0:T(8,128)S(1)}, bf1...) custom-call(bf16[384,768]{1,0:T(8,128)(2,1)S(1)} %get-tuple-element.111.refs_0_, bf16[384,768]{1,0:T(8,128)(2,1)S(1)} %copy-done.18, ...), custom_call_target="tpu_custom_call" | custom-call | flops 4600000000 | bytes 1024 | tf_op jit(solution)/shard_map/attn_grads/pallas_call | solution.py:702
  122.4 5.1 %token_bwd.1 = (f32[192,768]{1,0:T(8,128)S(1)}, f32[192,768]{1,0:T(8,128)S(1)}, bf16[384,768]{1,0:T(8,128)(2,1)S(1)}) custom-call(bf16[384,192]{1,0:T(8,128)(2,1)S(1)} %get-tuple-element.156.refs_4_.refs_0_, bf16[384,192]{1,0:T(8,128)(2,1)S(1)} %get-tuple-element.158.refs_6_.refs_1_, bf16[384,192]{1,0:T(8,128)(2,1)S(1)} %get-tuple-element.160.refs_8_.refs_2_, ...), custom_call_target="tpu_custom_call" | custom-call | flops 46000001024 | bytes 1024 | tf_op jit(solution)/shard_map/token_bwd/pallas_call | solution.py:702
  127.5 1.6 %collective-permute-done.24.came.one = bf16[288,768]{1,0:T(8,128)(2,1)S(1)} collective-permute-done((bf16[288,768]{1,0:T(8,128)(2,1)S(1)}, bf16[288,768]{1,0:T(8,128)(2,1)S(1)}, u32[]{:S(2)}, u32[]{:S(2)}) %collective-permute-start.24) | collective-permute-done | bytes 442400 | tf_op jit(solution)/shard_map/ppermute | solution.py:48
  131.1 2.5 %collective-permute-start.36 = (bf16[256,384]{1,0:T(8,128)(2,1)S(1)}, bf16[256,384]{1,0:T(8,128)(2,1)S(1)}, u32[]{:S(2)}, u32[]{:S(2)}) collective-permute-start(bf16[256,384]{1,0:T(8,128)(2,1)S(1)} %get-tuple-element.187), channel_id=1, source_target_pairs={{0,8},{4,12},{8,0},{12,4},{16,24},{20,28},{24,16},{28,20},{1,9},{5... | collective-permute-start | bytes 589832 | tf_op jit(solution)/shard_map/ppermute | solution.py:48
  134.6 4.2 %collective-permute-done.29.came = bf16[384,384]{1,0:T(8,128)(2,1)S(1)} collective-permute-done((bf16[384,384]{1,0:T(8,128)(2,1)S(1)}, bf16[384,384]{1,0:T(8,128)(2,1)S(1)}, u32[]{:S(2)}, u32[]{:S(2)}) %collective-permute-start.29) | collective-permute-done | bytes 294944 | tf_op jit(solution)/shard_map/ppermute | solution.py:48
  138.8 2.4 %collective-permute-start.31 = (bf16[192,384]{1,0:T(8,128)(2,1)S(1)}, bf16[192,384]{1,0:T(8,128)(2,1)S(1)}, u32[]{:S(2)}, u32[]{:S(2)}) collective-permute-start(bf16[192,384]{1,0:T(8,128)(2,1)S(1)} %get-tuple-element.173), channel_id=1, source_target_pairs={{0,8},{4,12},{8,0},{12,4},{16,24},{20,28},{24,16},{28,20},{1,9},{5... | collective-permute-start | bytes 442376 | tf_op jit(solution)/shard_map/ppermute | solution.py:48
  141.3 2.1 %collective-permute-start.37 = (bf16[128,384]{1,0:T(8,128)(2,1)S(1)}, bf16[128,384]{1,0:T(8,128)(2,1)S(1)}, u32[]{:S(2)}, u32[]{:S(2)}) collective-permute-start(bf16[128,384]{1,0:T(8,128)(2,1)S(1)} %get-tuple-element.190), channel_id=1, source_target_pairs={{0,16},{4,20},{8,24},{12,28},{16,0},{20,4},{24,8},{28,12},{1,17},{... | collective-permute-start | bytes 294920 | tf_op jit(solution)/shard_map/ppermute | solution.py:48
  144.3 1.5 collective-permute-start.35
  145.8 2.1 %collective-permute-done.37.refs_1_.late_came = bf16[128,384]{1,0:T(8,128)(2,1)S(1)} collective-permute-done((bf16[128,384]{1,0:T(8,128)(2,1)S(1)}, bf16[128,384]{1,0:T(8,128)(2,1)S(1)}, u32[]{:S(2)}, u32[]{:S(2)}) %collective-permute-start.37) | collective-permute-done | bytes 98336 | tf_op jit(solution)/shard_map/ppermute | solution.py:48
  150.0 1.6 %collective-permute-start.41 = (bf16[96,768]{1,0:T(8,128)(2,1)S(1)}, bf16[96,768]{1,0:T(8,128)(2,1)S(1)}, u32[]{:S(2)}, u32[]{:S(2)}) collective-permute-start(bf16[96,768]{1,0:T(8,128)(2,1)S(1)} %fold.1.late.refs_0_), channel_id=1, source_target_pairs={{0,2},{1,3},{2,0},{3,1},{4,6},{5,7},{6,4},{7,5},{8,10},{9,11},{10,... | collective-permute-start | bytes 442376 | tf_op jit(solution)/shard_map/ppermute | solution.py:48
  152.3 3.0 %collective-permute-done.38.refs_3_ = bf16[96,384]{1,0:T(8,128)(2,1)S(1)} collective-permute-done((bf16[96,384]{1,0:T(8,128)(2,1)S(1)}, bf16[96,384]{1,0:T(8,128)(2,1)S(1)}, u32[]{:S(2)}, u32[]{:S(2)}) %collective-permute-start.38) | collective-permute-done | bytes 73760 | tf_op jit(solution)/shard_map/ppermute | solution.py:48
  (121 shorter events, 21.2 us)
Async XLA Ops:
  2.5 11.1 %collective-permute-start.3 = (bf16[96,768]{1,0:T(8,128)(2,1)S(1)}, bf16[96,768]{1,0:T(8,128)(2,1)S(1)}, u32[]{:S(2)}, u32[]{:S(2)}) collective-permute-start(bf16[96,768]{1,0:T(8,128)(2,1)S(1)} %turn.1.refs_0_), channel_id=1, source_target_pairs={{0,16},{4,20},{8,24},{12,28},{16,0},{20,4},{24,8},{28,12},{1,17},{... | collective-permute-start | bytes 442376 | tf_op jit(solution)/shard_map/ppermute | solution.py:48
  6.6 9.3 %collective-permute-start.7 = (bf16[192,768]{1,0:T(8,128)(2,1)S(1)}, bf16[192,768]{1,0:T(8,128)(2,1)S(1)}, u32[]{:S(2)}, u32[]{:S(2)}) collective-permute-start(bf16[192,768]{1,0:T(8,128)(2,1)S(1)} %join.7), channel_id=1, source_target_pairs={{0,4},{4,0},{8,12},{12,8},{16,20},{20,16},{24,28},{28,24},{1,5},{5... | collective-permute-start | bytes 884744 | tf_op jit(solution)/shard_map/ppermute | solution.py:48
  8.2 11.2 %collective-permute-start.1 = (bf16[192,768]{1,0:T(8,128)(2,1)S(1)}, bf16[192,768]{1,0:T(8,128)(2,1)S(1)}, u32[]{:S(2)}, u32[]{:S(2)}) collective-permute-start(bf16[192,768]{1,0:T(8,128)(2,1)S(1)} %bitcast.18), channel_id=1, source_target_pairs={{0,2},{1,3},{2,0},{3,1},{4,6},{5,7},{6,4},{7,5},{8,10},{9,11},{10,... | collective-permute-start | bytes 884744 | tf_op jit(solution)/shard_map/ppermute | solution.py:48
  13.6 11.4 %collective-permute-start.4 = (bf16[192,768]{1,0:T(8,128)(2,1)S(1)}, bf16[192,768]{1,0:T(8,128)(2,1)S(1)}, u32[]{:S(2)}, u32[]{:S(2)}) collective-permute-start(bf16[192,768]{1,0:T(8,128)(2,1)S(1)} %join.6.rest_0_.refs_3_), channel_id=1, source_target_pairs={{0,8},{4,12},{8,0},{12,4},{16,24},{20,28},{24,16},{28,20},{1,9},{5... | collective-permute-start | bytes 884744 | tf_op jit(solution)/shard_map/ppermute | solution.py:48
  14.4 11.9 %collective-permute-start.5 = (bf16[192,768]{1,0:T(8,128)(2,1)S(1)}, bf16[192,768]{1,0:T(8,128)(2,1)S(1)}, u32[]{:S(2)}, u32[]{:S(2)}) collective-permute-start(bf16[192,768]{1,0:T(8,128)(2,1)S(1)} %join.6.rest_0_.refs_3_), channel_id=1, source_target_pairs={{0,4},{4,0},{8,12},{12,8},{16,20},{20,16},{24,28},{28,24},{1,5},{5... | collective-permute-start | bytes 884744 | tf_op jit(solution)/shard_map/ppermute | solution.py:48
  15.9 10.4 %collective-permute-start.8 = (bf16[96,768]{1,0:T(8,128)(2,1)S(1)}, bf16[96,768]{1,0:T(8,128)(2,1)S(1)}, u32[]{:S(2)}, u32[]{:S(2)}) collective-permute-start(bf16[96,768]{1,0:T(8,128)(2,1)S(1)} %gate.2.refs_0_), channel_id=1, source_target_pairs={{0,16},{4,20},{8,24},{12,28},{16,0},{20,4},{24,8},{28,12},{1,17},{... | collective-permute-start | bytes 442376 | tf_op jit(solution)/shard_map/ppermute | solution.py:48
  19.4 12.2 %collective-permute-start = (bf16[192,768]{1,0:T(8,128)(2,1)S(1)}, bf16[192,768]{1,0:T(8,128)(2,1)S(1)}, u32[]{:S(2)}, u32[]{:S(2)}) collective-permute-start(bf16[192,768]{1,0:T(8,128)(2,1)S(1)} %bitcast.19), channel_id=1, source_target_pairs={{0,1},{1,0},{2,3},{3,2},{4,5},{5,4},{6,7},{7,6},{8,9},{9,8},{10,11... | collective-permute-start | bytes 884744 | tf_op jit(solution)/shard_map/ppermute | solution.py:48
  19.4 12.2 %collective-permute-start.2 = (bf16[192,768]{1,0:T(8,128)(2,1)S(1)}, bf16[192,768]{1,0:T(8,128)(2,1)S(1)}, u32[]{:S(2)}, u32[]{:S(2)}) collective-permute-start(bf16[192,768]{1,0:T(8,128)(2,1)S(1)} %collective-permute-done.1.refs_2_), channel_id=1, source_target_pairs={{0,1},{1,0},{2,3},{3,2},{4,5},{5,4},{6,7},{7,6},{8,9},{9,8},{10,11... | collective-permute-start | bytes 884744 | tf_op jit(solution)/shard_map/ppermute | solution.py:48
  25.0 8.5 %collective-permute-start.6 = (bf16[192,768]{1,0:T(8,128)(2,1)S(1)}, bf16[192,768]{1,0:T(8,128)(2,1)S(1)}, u32[]{:S(2)}, u32[]{:S(2)}) collective-permute-start(bf16[192,768]{1,0:T(8,128)(2,1)S(1)} %collective-permute-done.4.refs_3_.refs_4_), channel_id=1, source_target_pairs={{0,4},{4,0},{8,12},{12,8},{16,20},{20,16},{24,28},{28,24},{1,5},{5... | collective-permute-start | bytes 884744 | tf_op jit(solution)/shard_map/ppermute | solution.py:48
  26.3 14.5 %collective-permute-start.9 = (bf16[192,768]{1,0:T(8,128)(2,1)S(1)}, bf16[192,768]{1,0:T(8,128)(2,1)S(1)}, u32[]{:S(2)}, u32[]{:S(2)}) collective-permute-start(bf16[192,768]{1,0:T(8,128)(2,1)S(1)} %join.8.refs_7_.rest_0_.refs_2_), channel_id=1, source_target_pairs={{0,8},{4,12},{8,0},{12,4},{16,24},{20,28},{24,16},{28,20},{1,9},{5... | collective-permute-start | bytes 884744 | tf_op jit(solution)/shard_map/ppermute | solution.py:48
  28.3 9.0 %collective-permute-start.10 = (bf16[96,768]{1,0:T(8,128)(2,1)S(1)}, bf16[96,768]{1,0:T(8,128)(2,1)S(1)}, u32[]{:S(2)}, u32[]{:S(2)}) collective-permute-start(bf16[96,768]{1,0:T(8,128)(2,1)S(1)} %gate.3.refs_0_), channel_id=1, source_target_pairs={{0,16},{4,20},{8,24},{12,28},{16,0},{20,4},{24,8},{28,12},{1,17},{... | collective-permute-start | bytes 442376 | tf_op jit(solution)/shard_map/ppermute | solution.py:48
  35.5 7.7 %collective-permute-start.11 = (bf16[384,768]{1,0:T(8,128)(2,1)S(1)}, bf16[384,768]{1,0:T(8,128)(2,1)S(1)}, u32[]{:S(2)}, u32[]{:S(2)}) collective-permute-start(bf16[384,768]{1,0:T(8,128)(2,1)S(1)} %get-tuple-element.115), channel_id=1, source_target_pairs={{0,1},{1,0},{2,3},{3,2},{4,5},{5,4},{6,7},{7,6},{8,9},{9,8},{10,11... | collective-permute-start | bytes 1769480 | tf_op jit(solution)/shard_map/ppermute | solution.py:48
  37.4 8.6 %collective-permute-start.14 = (bf16[192,768]{1,0:T(8,128)(2,1)S(1)}, bf16[192,768]{1,0:T(8,128)(2,1)S(1)}, u32[]{:S(2)}, u32[]{:S(2)}) collective-permute-start(bf16[192,768]{1,0:T(8,128)(2,1)S(1)} %join.9.refs_5_.rest_0_.refs_6_), channel_id=1, source_target_pairs={{0,8},{4,12},{8,0},{12,4},{16,24},{20,28},{24,16},{28,20},{1,9},{5... | collective-permute-start | bytes 884744 | tf_op jit(solution)/shard_map/ppermute | solution.py:48
  40.8 15.8 %collective-permute-start.13 = (bf16[288,768]{1,0:T(8,128)(2,1)S(1)}, bf16[288,768]{1,0:T(8,128)(2,1)S(1)}, u32[]{:S(2)}, u32[]{:S(2)}) collective-permute-start(bf16[288,768]{1,0:T(8,128)(2,1)S(1)} %join.10), channel_id=1, source_target_pairs={{0,4},{4,0},{8,12},{12,8},{16,20},{20,16},{24,28},{28,24},{1,5},{5... | collective-permute-start | bytes 1327112 | tf_op jit(solution)/shard_map/ppermute | solution.py:48
  43.3 12.6 %copy-start.11 = (f32[2,768]{1,0:T(2,128)S(1)}, f32[2,768]{1,0:T(2,128)}, u32[]{:S(2)}) copy-start(f32[2,768]{1,0:T(2,128)} %refs_3_.1) | copy-start | bytes 18436
  43.4 12.6 %collective-permute-start.12 = (bf16[384,768]{1,0:T(8,128)(2,1)S(1)}, bf16[384,768]{1,0:T(8,128)(2,1)S(1)}, u32[]{:S(2)}, u32[]{:S(2)}) collective-permute-start(bf16[384,768]{1,0:T(8,128)(2,1)S(1)} %chip_sum.3.mine), channel_id=1, source_target_pairs={{0,2},{1,3},{2,0},{3,1},{4,6},{5,7},{6,4},{7,5},{8,10},{9,11},{10,... | collective-permute-start | bytes 1769480 | tf_op jit(solution)/shard_map/ppermute | solution.py:48
  46.0 14.2 %collective-permute-start.15 = (bf16[288,768]{1,0:T(8,128)(2,1)S(1)}, bf16[288,768]{1,0:T(8,128)(2,1)S(1)}, u32[]{:S(2)}, u32[]{:S(2)}) collective-permute-start(bf16[288,768]{1,0:T(8,128)(2,1)S(1)} %join.11), channel_id=1, source_target_pairs={{0,4},{4,0},{8,12},{12,8},{16,20},{20,16},{24,28},{28,24},{1,5},{5... | collective-permute-start | bytes 1327112 | tf_op jit(solution)/shard_map/ppermute | solution.py:48
  56.6 5.7 %collective-permute-start.16 = (bf16[384,768]{1,0:T(8,128)(2,1)S(1)}, bf16[384,768]{1,0:T(8,128)(2,1)S(1)}, u32[]{:S(2)}, u32[]{:S(2)}) collective-permute-start(bf16[384,768]{1,0:T(8,128)(2,1)S(1)} %get-tuple-element.118.refs_0_), channel_id=1, source_target_pairs={{0,1},{1,0},{2,3},{3,2},{4,5},{5,4},{6,7},{7,6},{8,9},{9,8},{10,11... | collective-permute-start | bytes 1769480 | tf_op jit(solution)/shard_map/ppermute | solution.py:48
  64.3 2.1 %collective-permute-start.17 = (bf16[384,768]{1,0:T(8,128)(2,1)S(1)}, bf16[384,768]{1,0:T(8,128)(2,1)S(1)}, u32[]{:S(2)}, u32[]{:S(2)}) collective-permute-start(bf16[384,768]{1,0:T(8,128)(2,1)S(1)} %get-tuple-element.122), channel_id=1, source_target_pairs={{0,1},{1,0},{2,3},{3,2},{4,5},{5,4},{6,7},{7,6},{8,9},{9,8},{10,11... | collective-permute-start | bytes 1769480 | tf_op jit(solution)/shard_map/ppermute | solution.py:48
  66.5 15.4 %collective-permute-start.18 = (bf16[384,768]{1,0:T(8,128)(2,1)S(1)}, bf16[384,768]{1,0:T(8,128)(2,1)S(1)}, u32[]{:S(2)}, u32[]{:S(2)}) collective-permute-start(bf16[384,768]{1,0:T(8,128)(2,1)S(1)} %chip_sum.4.refs_1_), channel_id=1, source_target_pairs={{0,2},{1,3},{2,0},{3,1},{4,6},{5,7},{6,4},{7,5},{8,10},{9,11},{10,... | collective-permute-start | bytes 1769480 | tf_op jit(solution)/shard_map/ppermute | solution.py:48
  68.1 4.2 %collective-permute-start.19 = (bf16[4,8,768]{2,1,0:T(8,128)(2,1)S(1)}, bf16[4,8,768]{2,1,0:T(8,128)(2,1)S(1)}, u32[]{:S(2)}, u32[]{:S(2)}) collective-permute-start(bf16[4,8,768]{2,1,0:T(8,128)(2,1)S(1)} %get-tuple-element.124), channel_id=1, source_target_pairs={{0,4},{4,0},{8,12},{12,8},{16,20},{20,16},{24,28},{28,24},{1,5},{5... | collective-permute-start | bytes 147464 | tf_op jit(solution)/shard_map/ppermute | solution.py:48
  72.3 9.7 %copy-start.5 = (bf16[64,768]{1,0:T(8,128)(2,1)S(1)}, bf16[64,768]{1,0:T(8,128)(2,1)}, u32[]{:S(2)}) copy-start(bf16[64,768]{1,0:T(8,128)(2,1)} %refs_6_.1) | copy-start | bytes 294916
  72.3 9.7 %copy-start.13 = (bf16[8,64]{1,0:T(8,128)(2,1)S(1)}, bf16[8,64]{1,0:T(8,128)(2,1)}, u32[]{:S(2)}) copy-start(bf16[8,64]{1,0:T(8,128)(2,1)} %refs_8_.1) | copy-start | bytes 3076
  72.3 9.7 %copy-start.14 = (f32[64]{0:T(128)S(1)}, f32[64]{0:T(128)}, u32[]{:S(2)}) copy-start(f32[64]{0:T(128)} %param.28) | copy-start | bytes 772
  72.3 9.7 %copy-start.15 = (f32[8]{0:T(128)S(1)}, f32[8]{0:T(128)}, u32[]{:S(2)}) copy-start(f32[8]{0:T(128)} %param.30) | copy-start | bytes 100
  72.3 9.7 %copy-start.16 = (s32[8]{0:T(128)S(1)}, s32[8]{0:T(128)}, u32[]{:S(2)}) copy-start(s32[8]{0:T(128)} %refs_4_.5) | copy-start | bytes 100
  72.3 4.2 %collective-permute-start.20 = (bf16[4,8,768]{2,1,0:T(8,128)(2,1)S(1)}, bf16[4,8,768]{2,1,0:T(8,128)(2,1)S(1)}, u32[]{:S(2)}, u32[]{:S(2)}) collective-permute-start(bf16[4,8,768]{2,1,0:T(8,128)(2,1)S(1)} %get-tuple-element.126), channel_id=1, source_target_pairs={{0,8},{4,12},{8,0},{12,4},{16,24},{20,28},{24,16},{28,20},{1,9},{5... | collective-permute-start | bytes 147464 | tf_op jit(solution)/shard_map/ppermute | solution.py:48
  76.5 5.3 %collective-permute-start.21 = (bf16[4,8,768]{2,1,0:T(8,128)(2,1)S(1)}, bf16[4,8,768]{2,1,0:T(8,128)(2,1)S(1)}, u32[]{:S(2)}, u32[]{:S(2)}) collective-permute-start(bf16[4,8,768]{2,1,0:T(8,128)(2,1)S(1)} %pair_second.1), channel_id=1, source_target_pairs={{0,16},{4,20},{8,24},{12,28},{16,0},{20,4},{24,8},{28,12},{1,17},{... | collective-permute-start | bytes 147464 | tf_op jit(solution)/shard_map/ppermute | solution.py:48
  85.8 2.6 %collective-permute-start.22 = (bf16[672,768]{1,0:T(8,128)(2,1)S(1)}, bf16[672,768]{1,0:T(8,128)(2,1)S(1)}, u32[]{:S(2)}, u32[]{:S(2)}) collective-permute-start(bf16[672,768]{1,0:T(8,128)(2,1)S(1)} %get-tuple-element.127.refs_0_.refs_5_.g), channel_id=1, source_target_pairs={{0,1},{1,0},{2,3},{3,2},{4,5},{5,4},{6,7},{7,6},{8,9},{9,8},{10,11... | collective-permute-start | bytes 3096584 | tf_op jit(solution)/shard_map/ppermute | solution.py:48
  89.6 3.2 %collective-permute-start.25 = (bf16[384,768]{1,0:T(8,128)(2,1)S(1)}, bf16[384,768]{1,0:T(8,128)(2,1)S(1)}, u32[]{:S(2)}, u32[]{:S(2)}) collective-permute-start(bf16[384,768]{1,0:T(8,128)(2,1)S(1)} %get-tuple-element.142), channel_id=1, source_target_pairs={{0,1},{1,0},{2,3},{3,2},{4,5},{5,4},{6,7},{7,6},{8,9},{9,8},{10,11... | collective-permute-start | bytes 1769480 | tf_op jit(solution)/shard_map/ppermute | solution.py:48
  92.1 18.8 %collective-permute-start.23 = (bf16[480,768]{1,0:T(8,128)(2,1)S(1)}, bf16[480,768]{1,0:T(8,128)(2,1)S(1)}, u32[]{:S(2)}, u32[]{:S(2)}) collective-permute-start(bf16[480,768]{1,0:T(8,128)(2,1)S(1)} %get-tuple-element.130.rest_0_), channel_id=1, source_target_pairs={{0,4},{4,0},{8,12},{12,8},{16,20},{20,16},{24,28},{28,24},{1,5},{5... | collective-permute-start | bytes 2211848 | tf_op jit(solution)/shard_map/ppermute | solution.py:48
  93.0 15.4 %collective-permute-start.26 = (bf16[384,768]{1,0:T(8,128)(2,1)S(1)}, bf16[384,768]{1,0:T(8,128)(2,1)S(1)}, u32[]{:S(2)}, u32[]{:S(2)}) collective-permute-start(bf16[384,768]{1,0:T(8,128)(2,1)S(1)} %chip_sum.5.mine), channel_id=1, source_target_pairs={{0,2},{1,3},{2,0},{3,1},{4,6},{5,7},{6,4},{7,5},{8,10},{9,11},{10,... | collective-permute-start | bytes 1769480 | tf_op jit(solution)/shard_map/ppermute | solution.py:48
  95.8 15.7 %collective-permute-start.32 = (bf16[384,768]{1,0:T(8,128)(2,1)S(1)}, bf16[384,768]{1,0:T(8,128)(2,1)S(1)}, u32[]{:S(2)}, u32[]{:S(2)}) collective-permute-start(bf16[384,768]{1,0:T(8,128)(2,1)S(1)} %get-tuple-element.146.rest_0_.refs_9_), channel_id=1, source_target_pairs={{0,8},{4,12},{8,0},{12,4},{16,24},{20,28},{24,16},{28,20},{1,9},{5... | collective-permute-start | bytes 1769480 | tf_op jit(solution)/shard_map/ppermute | solution.py:48
  109.3 5.0 %collective-permute-start.27 = (bf16[384,768]{1,0:T(8,128)(2,1)S(1)}, bf16[384,768]{1,0:T(8,128)(2,1)S(1)}, u32[]{:S(2)}, u32[]{:S(2)}) collective-permute-start(bf16[384,768]{1,0:T(8,128)(2,1)S(1)} %get-tuple-element.147.g_own.refs_2_), channel_id=1, source_target_pairs={{0,1},{1,0},{2,3},{3,2},{4,5},{5,4},{6,7},{7,6},{8,9},{9,8},{10,11... | collective-permute-start | bytes 1769480 | tf_op jit(solution)/shard_map/ppermute | solution.py:48
  111.2 18.0 %collective-permute-start.24 = (bf16[288,768]{1,0:T(8,128)(2,1)S(1)}, bf16[288,768]{1,0:T(8,128)(2,1)S(1)}, u32[]{:S(2)}, u32[]{:S(2)}) collective-permute-start(bf16[288,768]{1,0:T(8,128)(2,1)S(1)} %get-tuple-element.135), channel_id=1, source_target_pairs={{0,8},{4,12},{8,0},{12,4},{16,24},{20,28},{24,16},{28,20},{1,9},{5... | collective-permute-start | bytes 1327112 | tf_op jit(solution)/shard_map/ppermute | solution.py:48
  111.7 22.0 %collective-permute-start.33 = (bf16[192,768]{1,0:T(8,128)(2,1)S(1)}, bf16[192,768]{1,0:T(8,128)(2,1)S(1)}, u32[]{:S(2)}, u32[]{:S(2)}) collective-permute-start(bf16[192,768]{1,0:T(8,128)(2,1)S(1)} %get-tuple-element.177), channel_id=1, source_target_pairs={{0,16},{4,20},{8,24},{12,28},{16,0},{20,4},{24,8},{28,12},{1,17},{... | collective-permute-start | bytes 884744 | tf_op jit(solution)/shard_map/ppermute | solution.py:48
  121.2 9.8 %collective-permute-start.30 = (bf16[448,384]{1,0:T(8,128)(2,1)S(1)}, bf16[448,384]{1,0:T(8,128)(2,1)S(1)}, u32[]{:S(2)}, u32[]{:S(2)}) collective-permute-start(bf16[448,384]{1,0:T(8,128)(2,1)S(1)} %get-tuple-element.166.refs_2_.refs_0_.refs_11_), channel_id=1, source_target_pairs={{0,4},{4,0},{8,12},{12,8},{16,20},{20,16},{24,28},{28,24},{1,5},{5... | collective-permute-start | bytes 1032200 | tf_op jit(solution)/shard_map/ppermute | solution.py:48
  127.5 16.8 %collective-permute-start.34 = (bf16[384,768]{1,0:T(8,128)(2,1)S(1)}, bf16[384,768]{1,0:T(8,128)(2,1)S(1)}, u32[]{:S(2)}, u32[]{:S(2)}) collective-permute-start(bf16[384,768]{1,0:T(8,128)(2,1)S(1)} %get-tuple-element.184), channel_id=1, source_target_pairs={{0,1},{1,0},{2,3},{3,2},{4,5},{5,4},{6,7},{7,6},{8,9},{9,8},{10,11... | collective-permute-start | bytes 1769480 | tf_op jit(solution)/shard_map/ppermute | solution.py:48
  129.3 16.6 %collective-permute-start.28 = (bf16[160,768]{1,0:T(8,128)(2,1)S(1)}, bf16[160,768]{1,0:T(8,128)(2,1)S(1)}, u32[]{:S(2)}, u32[]{:S(2)}) collective-permute-start(bf16[160,768]{1,0:T(8,128)(2,1)S(1)} %get-tuple-element.167), channel_id=1, source_target_pairs={{0,16},{4,20},{8,24},{12,28},{16,0},{20,4},{24,8},{28,12},{1,17},{... | collective-permute-start | bytes 737288 | tf_op jit(solution)/shard_map/ppermute | solution.py:48
  129.8 9.0 %collective-permute-start.29 = (bf16[384,384]{1,0:T(8,128)(2,1)S(1)}, bf16[384,384]{1,0:T(8,128)(2,1)S(1)}, u32[]{:S(2)}, u32[]{:S(2)}) collective-permute-start(bf16[384,384]{1,0:T(8,128)(2,1)S(1)} %get-tuple-element.168), channel_id=1, source_target_pairs={{0,4},{4,0},{8,12},{12,8},{16,20},{20,16},{24,28},{28,24},{1,5},{5... | collective-permute-start | bytes 884744 | tf_op jit(solution)/shard_map/ppermute | solution.py:48
  131.1 10.2 %collective-permute-start.36 = (bf16[256,384]{1,0:T(8,128)(2,1)S(1)}, bf16[256,384]{1,0:T(8,128)(2,1)S(1)}, u32[]{:S(2)}, u32[]{:S(2)}) collective-permute-start(bf16[256,384]{1,0:T(8,128)(2,1)S(1)} %get-tuple-element.187), channel_id=1, source_target_pairs={{0,8},{4,12},{8,0},{12,4},{16,24},{20,28},{24,16},{28,20},{1,9},{5... | collective-permute-start | bytes 589832 | tf_op jit(solution)/shard_map/ppermute | solution.py:48
  133.7 9.8 %collective-permute-start.39 = (bf16[96,768]{1,0:T(8,128)(2,1)S(1)}, bf16[96,768]{1,0:T(8,128)(2,1)S(1)}, u32[]{:S(2)}, u32[]{:S(2)}) collective-permute-start(bf16[96,768]{1,0:T(8,128)(2,1)S(1)} %get-tuple-element.194), channel_id=1, source_target_pairs={{0,4},{4,0},{8,12},{12,8},{16,20},{20,16},{24,28},{28,24},{1,5},{5... | collective-permute-start | bytes 442376 | tf_op jit(solution)/shard_map/ppermute | solution.py:48
  138.8 9.2 %collective-permute-start.31 = (bf16[192,384]{1,0:T(8,128)(2,1)S(1)}, bf16[192,384]{1,0:T(8,128)(2,1)S(1)}, u32[]{:S(2)}, u32[]{:S(2)}) collective-permute-start(bf16[192,384]{1,0:T(8,128)(2,1)S(1)} %get-tuple-element.173), channel_id=1, source_target_pairs={{0,8},{4,12},{8,0},{12,4},{16,24},{20,28},{24,16},{28,20},{1,9},{5... | collective-permute-start | bytes 442376 | tf_op jit(solution)/shard_map/ppermute | solution.py:48
  141.3 6.6 %collective-permute-start.37 = (bf16[128,384]{1,0:T(8,128)(2,1)S(1)}, bf16[128,384]{1,0:T(8,128)(2,1)S(1)}, u32[]{:S(2)}, u32[]{:S(2)}) collective-permute-start(bf16[128,384]{1,0:T(8,128)(2,1)S(1)} %get-tuple-element.190), channel_id=1, source_target_pairs={{0,16},{4,20},{8,24},{12,28},{16,0},{20,4},{24,8},{28,12},{1,17},{... | collective-permute-start | bytes 294920 | tf_op jit(solution)/shard_map/ppermute | solution.py:48
  144.3 11.9 %collective-permute-start.35 = (bf16[192,768]{1,0:T(8,128)(2,1)S(1)}, bf16[192,768]{1,0:T(8,128)(2,1)S(1)}, u32[]{:S(2)}, u32[]{:S(2)}) collective-permute-start(bf16[192,768]{1,0:T(8,128)(2,1)S(1)} %get-tuple-element.186), channel_id=1, source_target_pairs={{0,2},{1,3},{2,0},{3,1},{4,6},{5,7},{6,4},{7,5},{8,10},{9,11},{10,... | collective-permute-start | bytes 884744 | tf_op jit(solution)/shard_map/ppermute | solution.py:48
  148.0 2.0 %collective-permute-start.40 = (f32[48,768]{1,0:T(8,128)S(1)}, f32[48,768]{1,0:T(8,128)S(1)}, u32[]{:S(2)}, u32[]{:S(2)}) collective-permute-start(f32[48,768]{1,0:T(8,128)S(1)} %early_sum.1.own), channel_id=1, source_target_pairs={{0,1},{1,0},{2,3},{3,2},{4,5},{5,4},{6,7},{7,6},{8,9},{9,8},{10,11... | collective-permute-start | bytes 442376 | tf_op jit(solution)/shard_map/ppermute | solution.py:48
  148.1 7.2 %collective-permute-start.38 = (bf16[96,384]{1,0:T(8,128)(2,1)S(1)}, bf16[96,384]{1,0:T(8,128)(2,1)S(1)}, u32[]{:S(2)}, u32[]{:S(2)}) collective-permute-start(bf16[96,384]{1,0:T(8,128)(2,1)S(1)} %get-tuple-element.191), channel_id=1, source_target_pairs={{0,16},{4,20},{8,24},{12,28},{16,0},{20,4},{24,8},{28,12},{1,17},{... | collective-permute-start | bytes 221192 | tf_op jit(solution)/shard_map/ppermute | solution.py:48
  150.0 7.1 %collective-permute-start.41 = (bf16[96,768]{1,0:T(8,128)(2,1)S(1)}, bf16[96,768]{1,0:T(8,128)(2,1)S(1)}, u32[]{:S(2)}, u32[]{:S(2)}) collective-permute-start(bf16[96,768]{1,0:T(8,128)(2,1)S(1)} %fold.1.late.refs_0_), channel_id=1, source_target_pairs={{0,2},{1,3},{2,0},{3,1},{4,6},{5,7},{6,4},{7,5},{8,10},{9,11},{10,... | collective-permute-start | bytes 442376 | tf_op jit(solution)/shard_map/ppermute | solution.py:48
  (13 other events, 44.4 us)
